TPU v7x, 32 devices: a whole 2x2x4 slice. The times are simulated.
32 devices in a mesh: section: 2 (over core), expert: 4 (over y, x), shard: 4 (over z).
Axes of the slice: x: 2, y: 2, z: 4, core: 2. Of those that a mesh axis runs over, the one named last changes fastest.
Arguments:
- x_in: bfloat16 [2, 16, 256, 768], P(None, ('expert', 'shard')), may hold values from -6 to 6
- cotangent: float32 [2, 16, 256, 768], P(None, ('expert', 'shard')), may hold values from -6 to 6
- gate_prev: bfloat16 [2, 16, 256, 8], P(None, ('expert', 'shard')), may hold values from -4 to 4
- segments: int32 [2, 16, 256], P(None, ('expert', 'shard')), may hold values from 0 to 3, never falling along the last dimension, each value on 1 to 128 neighbouring positions
- routes: int32 [2, 2, 16, 256, 2], P('section', None, ('expert', 'shard')), may hold values from 0 to 7, all different within a row
- priority: int32 [2, 2, 16, 256], P('section', None, ('expert', 'shard')), may hold values from 0 to 255, each once within a row
- attn_qkv: bfloat16 [2, 768, 2304], P('section', ('expert', 'shard')), may hold values from -0.21875 to 0.21875
- attn_out: bfloat16 [2, 768, 768], P('section', ('expert', 'shard')), may hold values from -0.875 to 0.875
- router: bfloat16 [2, 768, 8], P('section', ('expert', 'shard')), may hold values from -0.15625 to 0.15625
- const_proj: bfloat16 [2, 768, 4], P('section', ('expert', 'shard')), may hold values from -0.21875 to 0.21875
- const_vec: bfloat16 [2, 768, 2], P('section', ('expert', 'shard')), may hold values from -5 to 5
- gains: bfloat16 [2, 768, 2], P('section', ('expert', 'shard')), may hold values from 0.5 to 1.5
- gate_mix: float32 [2, 8, 8], P('section'), may hold values from -2 to 2
- expert_in: bfloat16 [2, 4, 768, 4096], P('section', 'expert', 'shard'), may hold values from -0.21875 to 0.21875
- expert_out: bfloat16 [2, 4, 2048, 768], P('section', 'expert', 'shard'), may hold values from -0.25 to 0.25
Outputs:
- section_out: bfloat16 [2, 2, 16, 256, 768], P('section', None, ('expert', 'shard'))
- section_grad: float32 [2, 2, 16, 256, 768], P('section', None, ('expert', 'shard'))
- gate_grad: float32 [2, 2, 16, 256, 8], P('section', None, ('expert', 'shard'))
- attn_qkv_grad: float32 [2, 768, 2304], P('section', ('expert', 'shard'))
- attn_out_grad: float32 [2, 768, 768], P('section', ('expert', 'shard'))
- router_grad: float32 [2, 768, 8], P('section', ('expert', 'shard'))
- const_proj_grad: float32 [2, 768, 4], P('section', ('expert', 'shard'))
- const_vec_grad: float32 [2, 768, 2], P('section', ('expert', 'shard'))
- gains_grad: float32 [2, 768, 2], P('section', ('expert', 'shard'))
- gate_mix_grad: float32 [2, 8, 8], P('section')
- expert_in_grad: float32 [2, 4, 768, 4096], P('section', 'expert', 'shard')
- expert_out_grad: float32 [2, 4, 2048, 768], P('section', 'expert', 'shard')
Inputs may be any that keep to these rules, and one draw needn't show every extreme that they name: `routes`: the 2 experts of a token differ; indices below 4 are feed-forward experts, then the zero, the copy and the 2 constant experts. `priority`: each sequence's tokens hold each number once. `segments`: segment numbers never fall along a sequence.
All inputs are finite; a program needn't handle non-finite values.
Results may differ from a plain program's by a relative error of at most 0.024.
Values may be sent and summed in bfloat16 or wider, within the bound.
A program may use at most 256 MiB of HBM per device.

v0:
```python
import math
import types

import jax
import jax.numpy as jnp
from jax import lax
from jax.experimental import pallas as pl
from jax.experimental.pallas import tpu as pltpu
from jax.sharding import PartitionSpec as P

HEADS = 12
HEAD = 64
TOP = 2
CHUNK = 256
LANES = 128
AT_PROJ = 16
AT_VEC = 24
AT_GAIN = 28
AT_MIX = 32

HIGH = lax.Precision.HIGHEST
norm_eps = 1e-06
masked_score = -1e30
F32 = jnp.float32
BF16 = jnp.bfloat16


VMEM_BYTES = 60 * 1024 * 1024


def mm(a, b, contract=((1,), (0,)), precision=None):
    return lax.dot_general(a, b, (contract, ((), ())), precision=precision, preferred_element_type=F32)


NT = ((1,), (1,))
TN = ((0,), (0,))


def lane_of(rows, columns=LANES):
    return lax.broadcasted_iota(jnp.int32, (rows, columns), 1)


def inverse_norm(values):
    return lax.rsqrt(jnp.mean(values * values, axis=-1, keepdims=True) + norm_eps)


def norm_back(grad_unit, unit, inverse):
    return inverse * (grad_unit - unit * jnp.mean(grad_unit * unit, axis=-1, keepdims=True))


def roll(x, by):
    return pltpu.roll(x, by, 1)


def turned(x, lane):
    return jnp.where(lane % HEAD < HEAD // 2, roll(x, LANES - HEAD // 2), roll(x, HEAD // 2))


def hi_lo(x):
    high = x.astype(BF16)
    return high, (x - high.astype(F32)).astype(BF16)


def ones_where(condition):
    return jnp.where(condition, 1.0, 0.0).astype(BF16)


def small_rows_of(small):
    rows = small[...].astype(F32).T
    return rows[AT_GAIN : AT_GAIN + 1], rows[AT_GAIN + 1 : AT_GAIN + 2], rows[AT_VEC:AT_GAIN]


def attention(x, w, gain_first, cosine, sine, seg_col, seg_row, qkv, probs_att, attended):
    seq_len, width = x.shape
    first_b = (x * inverse_norm(x) * gain_first).astype(BF16)
    place_q = lax.broadcasted_iota(jnp.int32, (seq_len, seq_len), 0)
    place_k = lax.broadcasted_iota(jnp.int32, (seq_len, seq_len), 1)
    bias = jnp.where((seg_col == seg_row) & (place_k <= place_q), 0.0, masked_score)
    lane = lane_of(seq_len)
    low_head = lane < HEAD
    for pair in range(width // LANES):
        at = pair * LANES
        q = mm(first_b, w[:, at : at + LANES])
        k = mm(first_b, w[:, width + at : width + at + LANES])
        v = mm(first_b, w[:, 2 * width + at : 2 * width + at + LANES]).astype(BF16)
        q = q * cosine + turned(q, lane) * sine
        k = (k * cosine + turned(k, lane) * sine).astype(BF16)
        outs = []
        for half in range(2):
            one = jnp.where(low_head if half == 0 else lane >= HEAD, q, 0.0).astype(BF16)
            scores = mm(one, k, NT) * (HEAD**-0.5) + bias
            scores = jnp.exp(scores - jnp.max(scores, axis=-1, keepdims=True))
            probs = (scores * (1.0 / jnp.sum(scores, axis=-1, keepdims=True))).astype(BF16)
            probs_att[2 * pair + half] = probs
            outs.append(mm(probs, v))
        attended[:, at : at + LANES] = jnp.where(low_head, outs[0], outs[1]).astype(BF16)
        qkv[:, at : at + LANES] = q.astype(BF16)
        qkv[:, width + at : width + at + LANES] = k
        qkv[:, 2 * width + at : 2 * width + at + LANES] = v
    return x + mm(attended[...], w[:, 3 * width : 4 * width])


def gating(after, r, small, mix, gain_second, ints, prio_row, dims, packed_ref, slot_ref, r_next, buffer):
    nffn, nexp, capacity, slots, _ = dims
    rows = after.shape[0]
    second_b = (after * inverse_norm(after) * gain_second).astype(BF16)
    lane = lane_of(rows)
    logits = mm(second_b, small)
    full = logits + mm(r, mix, precision=HIGH)
    inside = lane < nexp
    full = jnp.where(inside, full, masked_score)
    raised = jnp.exp(full - jnp.max(full, axis=-1, keepdims=True))
    probs = raised / jnp.sum(raised, axis=-1, keepdims=True)
    other = jnp.where(lane % 2 == 0, roll(logits, LANES - 1), roll(logits, 1))
    bigger = jnp.maximum(logits, other)
    mine_e = jnp.exp(logits - bigger)
    mixes = mine_e / (mine_e + jnp.exp(other - bigger))
    before = ones_where(prio_row < column_of(prio_row).astype(jnp.int32))
    route = (ints[:, 0:1], ints[:, 1:2])
    routed = ones_where(((lane == route[0]) | (lane == route[1])) & (lane < nffn))
    rank = mm(before, routed)
    gates, places = [], []
    dispatch = 0.0
    stride = slots // nffn
    for k in range(TOP):
        chosen = lane == route[k]
        gates.append(jnp.sum(jnp.where(chosen, probs, 0.0), axis=-1, keepdims=True))
        rank_k = jnp.sum(jnp.where(chosen, rank, 0.0), axis=-1, keepdims=True).astype(jnp.int32)
        kept = (route[k] < nffn) & (rank_k < capacity)
        places.append(jnp.where(kept, route[k] * stride + rank_k, -1))
        dispatch = dispatch + jnp.where(places[k] == lane_of(rows, slots), 1.0, 0.0)
    buffer[...] = mm(dispatch.astype(BF16), second_b, TN).astype(BF16).reshape(buffer.shape)
    packed = jnp.where(inside, probs, jnp.where((lane >= AT_PROJ) & (lane < AT_VEC), mixes, 0.0))
    packed = jnp.where(lane == AT_VEC, gates[0], packed)
    packed_ref[...] = jnp.where(lane == AT_VEC + 1, gates[1], packed)
    slot_ref[...] = jnp.where(lane == 0, places[0], places[1])
    if r_next is not None:
        r_next[...] = jnp.where(inside, full, 0.0).astype(BF16)


def extras(packed, ints, nffn, nconst):
    gates = (packed[:, AT_VEC : AT_VEC + 1], packed[:, AT_VEC + 1 : AT_VEC + 2])

    def of(expert):
        return sum(jnp.where(ints[:, k : k + 1] == expert, gates[k], 0.0) for k in range(TOP))

    def mixes(c):
        at = AT_PROJ + 2 * c
        return packed[:, at : at + 1], packed[:, at + 1 : at + 2]

    return gates, of(nffn + 1), [of(nffn + 2 + c) for c in range(nconst)], [mixes(c) for c in range(nconst)]


def combine(after, packed, slot_pair, ints, blocks, gain_second, vec_rows, dims, picked_ref):
    nffn, nexp, _, slots, _ = dims
    nconst = nexp - nffn - 2
    rows = after.shape[0]
    second = after * inverse_norm(after) * gain_second
    gates, copied, const, mixes = extras(packed, ints, nffn, nconst)
    made = blocks[...].reshape(slots, after.shape[1])
    slot_lane = lane_of(rows, slots)
    coefficient = copied
    for c in range(nconst):
        coefficient = coefficient + const[c] * mixes[c][0]
    out = after + coefficient * second
    for k in range(TOP):
        picked = mm(ones_where(slot_pair[:, k : k + 1] == slot_lane), made)
        picked_ref[k] = picked.astype(BF16)
        out = out + gates[k] * picked
    for c in range(nconst):
        out = out + (const[c] * mixes[c][1]) * vec_rows[c : c + 1]
    return out


def give_back(grad_y, packed, slot_pair, dims, buffer):
    slots = dims[3]
    slot_lane = lane_of(grad_y.shape[0], slots)
    total = 0.0
    for k in range(TOP):
        gate = packed[:, AT_VEC + k : AT_VEC + k + 1]
        table = ones_where(slot_pair[:, k : k + 1] == slot_lane)
        total = total + mm(table, (gate * grad_y).astype(BF16), TN)
    buffer[...] = total.astype(BF16).reshape(buffer.shape)


def moe_back(
    grad_y, grad_log_in, after, packed, slot_pair, ints, picked, blocks, r, small, mix, gain_second, vec_rows, dims
):
    nffn, nexp, _, slots, _ = dims
    nconst = nexp - nffn - 2
    rows = grad_y.shape[0]
    lane = lane_of(rows)
    inverse = inverse_norm(after)
    unit = after * inverse
    second = unit * gain_second
    second_b = second.astype(BF16)
    gates, copied, const, mixes = extras(packed, ints, nffn, nconst)
    grad_buffer = blocks[...].reshape(slots, after.shape[1])
    slot_lane = lane_of(rows, slots)
    dispatch = sum(jnp.where(slot_pair[:, k : k + 1] == slot_lane, 1.0, 0.0) for k in range(TOP))
    grad_second = mm(dispatch.astype(BF16), grad_buffer)
    along_second = jnp.sum(grad_y * second, axis=-1, keepdims=True)
    coefficient = copied
    grad_extra = [(nffn + 1, along_second)]
    grad_lanes = jnp.zeros((rows, LANES), F32)
    vec_grads = []
    for c in range(nconst):
        along = jnp.sum(grad_y * vec_rows[c : c + 1], axis=-1, keepdims=True)
        m0, m1 = mixes[c]
        coefficient = coefficient + const[c] * m0
        grad_extra.append((nffn + 2 + c, m0 * along_second + m1 * along))
        d0, d1 = const[c] * along_second, const[c] * along
        mean = m0 * d0 + m1 * d1
        at = AT_PROJ + 2 * c
        grad_lanes = jnp.where(lane == at, m0 * (d0 - mean), grad_lanes)
        grad_lanes = jnp.where(lane == at + 1, m1 * (d1 - mean), grad_lanes)
        vec_grads.append(jnp.sum(grad_y * (const[c] * m1), axis=0, keepdims=True))
    grad_second = grad_second + coefficient * grad_y
    grad_probs = jnp.zeros((rows, LANES), F32)
    for k in range(TOP):
        grad_gate = jnp.sum(picked[k].astype(F32) * grad_y, axis=-1, keepdims=True)
        for expert, value in grad_extra:
            grad_gate = grad_gate + jnp.where(ints[:, k : k + 1] == expert, value, 0.0)
        grad_probs = grad_probs + jnp.where(lane == ints[:, k : k + 1], grad_gate, 0.0)
    probs = jnp.where(lane < nexp, packed, 0.0)
    grad_logits = probs * (grad_probs - jnp.sum(probs * grad_probs, axis=-1, keepdims=True)) + grad_log_in
    grad_mix = mm(jnp.where(lane < nexp, r, 0.0), jnp.where(lane < nexp, grad_logits, 0.0), TN, HIGH)
    grad_r = mm(grad_logits, mix, NT, HIGH)
    high, low = hi_lo(jnp.where(lane < nexp, grad_logits, grad_lanes))
    small_rows = mm(high, second_b, TN) + mm(low, second_b, TN)
    grad_second = grad_second + mm(high, small, NT) + mm(low, small, NT)
    grad_gain = jnp.sum(grad_second * unit, axis=0, keepdims=True)
    grad_after = grad_y + norm_back(grad_second * gain_second, unit, inverse)
    row = lax.broadcasted_iota(jnp.int32, small_rows.shape, 0)
    small_rows = jnp.where(row < AT_VEC, small_rows, 0.0)
    for c in range(nconst):
        small_rows = jnp.where(row == AT_VEC + c, vec_grads[c], small_rows)
    small_rows = jnp.where(row == AT_GAIN + 1, grad_gain, small_rows)
    return grad_after, grad_r, grad_mix, small_rows


def attention_back(
    grad_after, x, qkv, probs_att, attended, small_rows, mix_tile, w, gain_first, cosine, sine, grads, grad_qkv, grad_x, hooks
):
    seq_len, width = x.shape
    inverse = inverse_norm(x)
    unit = x * inverse
    first_b = (unit * gain_first).astype(BF16)
    grad_branch = grad_after.astype(BF16)
    lane = lane_of(seq_len)
    low_head = lane < HEAD
    masks = (ones_where(low_head), ones_where(lane >= HEAD))
    scale = HEAD**-0.5
    heads_half = width // LANES // 2
    wide = heads_half * LANES

    def weight_grads(batch):
        for part in range(3):
            columns = slice(part * width + batch * wide, part * width + (batch + 1) * wide)
            grads[batch][:, part * wide : (part + 1) * wide] = mm(first_b, grad_qkv[:, columns], TN).astype(BF16)
        if batch == 0:
            grads[0][:, 3 * wide :] = mm(attended[...], grad_branch, TN).astype(BF16)

    for pair in range(width // LANES):
        at = pair * LANES
        q = qkv[:, at : at + LANES]
        k = qkv[:, width + at : width + at + LANES]
        v = qkv[:, 2 * width + at : 2 * width + at + LANES]
        g = mm(grad_branch, w[at : at + LANES, 3 * width : 4 * width], NT).astype(BF16)
        dq, dk, dv = [], [], []
        for half in range(2):
            probs = probs_att[2 * pair + half]
            grad_p = mm(g * masks[half], v, NT)
            p = probs.astype(F32)
            grad_s = (p * (grad_p - jnp.sum(p * grad_p, axis=-1, keepdims=True))).astype(BF16)
            dv.append(mm(probs, g, TN))
            dq.append(mm(grad_s, k))
            dk.append(mm(grad_s, q, TN))
        dq = jnp.where(low_head, dq[0], dq[1]) * scale
        dk = jnp.where(low_head, dk[0], dk[1]) * scale
        grad_qkv[:, at : at + LANES] = (dq * cosine - turned(dq, lane) * sine).astype(BF16)
        grad_qkv[:, width + at : width + at + LANES] = (dk * cosine - turned(dk, lane) * sine).astype(BF16)
        grad_qkv[:, 2 * width + at : 2 * width + at + LANES] = jnp.where(low_head, dv[0], dv[1]).astype(BF16)
        if hooks.early and pair == heads_half - 1:
            weight_grads(0)
            hooks.first_done()
    if hooks.early:
        hooks.heads_done()
        weight_grads(1)
    grad_first = mm(grad_qkv[...], w[:, : 3 * width], NT)
    grad_gain = jnp.sum(grad_first * unit, axis=0, keepdims=True)
    grad_x[...] = grad_after + norm_back(grad_first * gain_first, unit, inverse)
    row = lax.broadcasted_iota(jnp.int32, small_rows.shape, 0)
    small_rows = jnp.where(row == AT_GAIN, grad_gain, small_rows)
    grads[1][:, 3 * wide :] = (small_rows.T + mix_tile).astype(BF16)
    if not hooks.early:
        hooks.rows_done()
        weight_grads(0)
        hooks.first_done()
        weight_grads(1)
    hooks.second_done()


def attend_kernel(
    dims, x, r, w, small, mix, cosine, sine, seg_col, seg_row, ints, prio_row,
    after, qkv, probs_att, attended, packed, slot_pair, r_next, buffer,
):
    gain_first, gain_second, _ = small_rows_of(small)
    after_v = attention(
        x[...].astype(F32), w, gain_first, cosine[...], sine[...], seg_col, seg_row, qkv, probs_att, attended
    )
    after[...] = after_v
    gating(
        after_v, r[...].astype(F32), small[...], mix[...], gain_second, ints[...], prio_row[...], dims,
        packed, slot_pair, r_next, buffer,
    )


def middle_kernel(
    dims, after_0, packed_0, slots_0, ints_0, blocks_0, small_0,
    r, w, small, mix, cosine, sine, seg_col, seg_row, ints, prio_row, grad_y,
    out, picked, after, qkv, probs_att, attended, packed, slot_pair, buffer, grad_buffer,
):
    _, gain_second, vec_rows = small_rows_of(small_0)
    out[...] = combine(
        after_0[...], packed_0[...], slots_0[...], ints_0[...], blocks_0, gain_second, vec_rows, dims, picked
    ).astype(BF16)
    attend_kernel(
        dims, out, r, w, small, mix, cosine, sine, seg_col, seg_row, ints, prio_row,
        after, qkv, probs_att, attended, packed, slot_pair, None, buffer,
    )
    give_back(grad_y[...], packed[...], slot_pair[...], dims, grad_buffer)


def back_body(
    dims, grad_y, grad_log, after, packed, slot_pair, ints, picked, blocks, r, w, small, mix, x, qkv, probs_att, attended,
    cosine, sine, grad_x, grad_r, grad_mix, grads, grad_qkv, loading, hooks,
):
    gain_first, gain_second, vec_rows = small_rows_of(small)
    grad_log_v = 0.0 if grad_log is None else grad_log[...].astype(BF16).astype(F32)
    grad_y_v = grad_y[...] if grad_log is None else grad_y[...].astype(BF16).astype(F32)
    grad_after, grad_r_v, grad_mix_v, small_rows = moe_back(
        grad_y_v, grad_log_v, after[...], packed[...], slot_pair[...], ints[...], picked,
        blocks, r[...].astype(F32), small[...], mix[...], gain_second, vec_rows, dims,
    )
    grad_r[...] = grad_r_v
    grad_mix[...] = grad_mix_v
    rows = dims[4]
    mix_tile = 0.0
    if rows:
        mix_tile = jnp.concatenate([roll(grad_mix_v, AT_MIX)[:rows]] * (x.shape[1] // rows), axis=0)
    loading.wait()
    attention_back(
        grad_after, x[...].astype(F32), qkv, probs_att, attended, small_rows, mix_tile, w, gain_first,
        cosine[...], sine[...], grads, grad_qkv, grad_x, hooks,
    )


def shaped(shape, dtype):
    return jax.ShapeDtypeStruct(shape, dtype)


def call(kernel, identity, ins, outs, scratch, far, flops):
    groups = {name: value if isinstance(value, list) else None for name, value in scratch.items()}
    flat = []
    for value in scratch.values():
        flat += value if isinstance(value, list) else [value]

    def body(*refs):
        refs = list(refs)
        named = {name: refs.pop(0) for name in list(ins) + list(outs)}
        for name, group in groups.items():
            named[name] = refs.pop(0) if group is None else [refs.pop(0) for _ in group]
        kernel(types.SimpleNamespace(**named))

    def spaces(names):
        return [pl.BlockSpec(memory_space=pl.ANY if name in far else pltpu.VMEM) for name in names]

    got = pl.pallas_call(
        body,
        out_shape=list(outs.values()),
        in_specs=spaces(ins),
        out_specs=spaces(outs),
        scratch_shapes=flat,
        compiler_params=pltpu.CompilerParams(
            vmem_limit_bytes=VMEM_BYTES, collective_id=identity, has_side_effects=True
        ),
        cost_estimate=pl.CostEstimate(flops=flops, bytes_accessed=40 << 20, transcendentals=0),
    )(*ins.values())
    return types.SimpleNamespace(**dict(zip(outs, got)))


MESH = pl.DeviceIdType.MESH


class Exchange:
    def __init__(self, stream, sent, groups, partial, sibling_part, onward, pair_part, summed, result, sems):
        self.stream, self.sent, self.groups = stream, sent, groups
        self.partial, self.sibling_part, self.onward = partial, sibling_part, onward
        self.pair_part, self.summed, self.result = pair_part, summed, result
        (self.column_s, self.column_r, self.pair_s, self.pair_r, self.core_s, self.core_r, self.last_s, self.last_r,
         self.local_sem, self.back_s, self.back_r, self.far_s, self.far_r, self.over_s, self.over_r,
         self.home_s, self.home_r) = sems
        self.core, self.column, self.place = lax.axis_index("section"), lax.axis_index("expert"), lax.axis_index("shard")
        self.owners = lax.axis_size("expert")
        self.sibling = (1 - self.core, self.column, self.place)
        self.pair = (self.core, self.column, self.place + 1 - 2 * lax.rem(self.place, 2))

    def peer(self, column):
        return (self.core, column, self.place)

    def turn(self, by):
        return lax.rem(self.column + by + self.owners, self.owners)

    def to_column(self, by):
        return pltpu.make_async_remote_copy(
            self.sent.at[self.turn(by)], self.groups.at[0, self.column],
            self.column_s.at[self.stream, by], self.column_r.at[self.stream, by],
            device_id=self.peer(self.turn(by)), device_id_type=MESH,
        )

    def from_column(self, by):
        source = self.turn(-by)
        return pltpu.make_async_remote_copy(
            self.sent.at[source], self.groups.at[0, source],
            self.column_s.at[self.stream, by], self.column_r.at[self.stream, by],
            device_id=self.peer(source), device_id_type=MESH,
        )

    def own_block(self):
        return pltpu.make_async_copy(
            self.sent.at[self.column], self.groups.at[0, self.column], self.local_sem.at[self.stream]
        )

    def forward(self, by, here, there, device, send, recv):
        block = self.turn(-by)
        return pltpu.make_async_remote_copy(
            self.groups.at[here, block], self.groups.at[there, block],
            send.at[self.stream, by], recv.at[self.stream, by], device_id=device, device_id_type=MESH,
        )

    def to_pair(self, by):
        return self.forward(by, 0, 2, self.pair, self.pair_s, self.pair_r)

    def to_core(self, by):
        return self.forward(by, 0, 1, self.sibling, self.core_s, self.core_r)

    def to_core_last(self, by):
        return self.forward(by, 2, 3, self.sibling, self.last_s, self.last_r)

    def start(self):
        for by in range(1, self.owners):
            self.to_column(by).start()
        self.own_block().start()

    def spread(self):
        for by in range(self.owners):
            if by:
                self.from_column(by).wait_recv()
            else:
                self.own_block().wait()
            self.to_pair(by).start()
            self.to_core(by).start()

    def near_ready(self):
        for by in range(self.owners):
            self.to_core(by).wait_recv()

    def spread_far(self, bys):
        for by in bys:
            self.to_pair(by).wait_recv()
            self.to_core_last(by).start()

    def far_ready(self, bys):
        for by in bys:
            self.to_core_last(by).wait_recv()

    def finish_dispatch(self):
        for by in range(self.owners):
            if by:
                self.to_column(by).wait_send()
            self.to_pair(by).wait_send()
            self.to_core(by).wait_send()
            self.to_core_last(by).wait_send()

    def near_back(self):
        return pltpu.make_async_remote_copy(
            self.partial.at[1], self.sibling_part.at[0], self.back_s.at[self.stream], self.back_r.at[self.stream],
            device_id=self.sibling, device_id_type=MESH,
        )

    def far_back(self, by):
        block = self.turn(-by)
        return pltpu.make_async_remote_copy(
            self.partial.at[3, block], self.sibling_part.at[1, block],
            self.far_s.at[self.stream, by], self.far_r.at[self.stream, by],
            device_id=self.sibling, device_id_type=MESH,
        )

    def over_pair(self, by):
        block = self.turn(-by)
        return pltpu.make_async_remote_copy(
            self.onward.at[block], self.pair_part.at[block],
            self.over_s.at[self.stream, by], self.over_r.at[self.stream, by],
            device_id=self.pair, device_id_type=MESH,
        )

    def home(self, by):
        return pltpu.make_async_remote_copy(
            self.summed.at[self.turn(by)], self.result.at[self.column],
            self.home_s.at[self.stream, by], self.home_r.at[self.stream, by],
            device_id=self.peer(self.turn(by)), device_id_type=MESH,
        )

    def home_here(self, by):
        source = self.turn(-by)
        return pltpu.make_async_remote_copy(
            self.summed.at[source], self.result.at[source],
            self.home_s.at[self.stream, by], self.home_r.at[self.stream, by],
            device_id=self.peer(source), device_id_type=MESH,
        )

    def return_far(self, bys):
        for by in bys:
            block = self.turn(-by)
            self.far_back(by).wait_recv()
            total = self.partial[2, block].astype(F32) + self.sibling_part[1, block].astype(F32)
            self.onward[block] = total.astype(BF16)
            self.over_pair(by).start()

    def return_home(self, bys):
        for by in bys:
            block = self.turn(-by)
            near = self.partial[0, block].astype(F32) + self.sibling_part[0, block].astype(F32)
            self.over_pair(by).wait_recv()
            self.summed[block] = (near + self.pair_part[block].astype(F32)).astype(BF16)
            if by:
                self.home(self.owners - by).start()
            else:
                self.result[block] = self.summed[block]

    def near_arrived(self):
        self.near_back().wait_recv()

    def finish(self):
        for by in range(1, self.owners):
            self.home_here(by).wait_recv()
            self.home(by).wait_send()
        for by in range(self.owners):
            self.over_pair(by).wait_send()
            self.far_back(by).wait_send()
        self.near_back().wait_send()

    def steps(self):
        cut = self.owners // 2
        return [list(range(cut)), list(range(cut, self.owners))]

    def far(self, bys):
        return [(group, self.turn(-by)) for by in bys for group in (2, 3)]


def home_buffers(owners, room, width):
    block = (owners, room, width)
    return [pltpu.VMEM((4,) + block, BF16), pltpu.VMEM((2,) + block, BF16)] + [pltpu.VMEM(block, BF16)] * 3


def exchange_sems(streams, owners):
    dma = pltpu.SemaphoreType.DMA
    return [dma((streams, owners))] * 8 + [dma((streams,))] * 3 + [dma((streams, owners))] * 6


def near_rows(ref):
    groups, owners, room, width = ref.shape
    return ref[:2].reshape(2 * owners * room, width)


def put_near(ref, value, columns=slice(None)):
    groups, owners, room, _ = ref.shape
    ref[:2, :, :, columns] = value.astype(ref.dtype).reshape(2, owners, room, value.shape[1])


def rows_at(ref, picks, columns=slice(None)):
    return jnp.concatenate([ref[group, block, :, columns] for group, block in picks], axis=0)


def put_at(ref, picks, value, columns=slice(None)):
    room = ref.shape[2]
    for i, (group, block) in enumerate(picks):
        ref[group, block, :, columns] = value[i * room : (i + 1) * room].astype(ref.dtype)


def all_rows(ref):
    groups, owners, room, width = ref.shape
    return ref[...].reshape(groups * owners * room, width)


def chunks_of(w_out):
    for chunk in range(w_out.shape[0] // CHUNK):
        yield slice(2 * CHUNK * chunk, 2 * CHUNK * (chunk + 1)), slice(CHUNK * chunk, CHUNK * (chunk + 1))


def made_by(rows, w_in, w_out):
    total = 0.0
    for columns, units in chunks_of(w_out):
        both = mm(rows, w_in[:, columns])
        gate = both[:, :CHUNK]
        hidden = (gate * jax.nn.sigmoid(gate) * both[:, CHUNK:]).astype(BF16)
        total = total + mm(hidden, w_out[units])
    return total


def forward_again(rows, w_in, w_out, put_both, put_hidden):
    for columns, units in chunks_of(w_out):
        both = mm(rows, w_in[:, columns])
        gate = both[:, :CHUNK]
        put_both(both, columns)
        put_hidden(gate * jax.nn.sigmoid(gate) * both[:, CHUNK:], units)


def back_of(grad_rows, w_in, w_out, both_at, put_grad):
    total = 0.0
    for columns, units in chunks_of(w_out):
        both = both_at(columns).astype(F32)
        gate, up = both[:, :CHUNK], both[:, CHUNK:]
        sig = jax.nn.sigmoid(gate)
        grad_hidden = mm(grad_rows, w_out[units], NT)
        grad_gate = grad_hidden * up * sig * (1.0 + gate * (1.0 - sig))
        grad_both = jnp.concatenate([grad_gate, grad_hidden * gate * sig], axis=1).astype(BF16)
        put_grad(grad_both, columns)
        total = total + mm(grad_both, w_in[:, columns], NT)
    return total


def both_ways(rows, grad_rows, w_in, w_out, put_hidden, put_grad):
    made, back = 0.0, 0.0
    for columns, units in chunks_of(w_out):
        both = mm(rows, w_in[:, columns])
        gate, up = both[:, :CHUNK], both[:, CHUNK:]
        sig = jax.nn.sigmoid(gate)
        hidden = (gate * sig * up).astype(BF16)
        put_hidden(hidden, units)
        made = made + mm(hidden, w_out[units])
        grad_hidden = mm(grad_rows, w_out[units], NT)
        grad_gate = grad_hidden * up * sig * (1.0 + gate * (1.0 - sig))
        grad_both = jnp.concatenate([grad_gate, grad_hidden * gate * sig], axis=1).astype(BF16)
        put_grad(grad_both, columns)
        back = back + mm(grad_both, w_in[:, columns], NT)
    return made, back


def near_of(ref):
    return lambda value, columns: put_near(ref, value, columns)


def far_of(ref, picks):
    return lambda value, columns: put_at(ref, picks, value, columns)


def weight_grads_in(rows, grad_ref, grad_in):
    for chunk in range(grad_in.shape[1] // (2 * CHUNK)):
        columns = slice(2 * CHUNK * chunk, 2 * CHUNK * (chunk + 1))
        grads = grad_ref[:, :, :, columns].reshape(rows.shape[0], 2 * CHUNK)
        grad_in[:, columns] = mm(rows, grads, TN).astype(BF16)


def exchange_far(streams, work):
    first, then = streams[0].steps()
    for bys in (first, then):
        for one in streams:
            one.spread_far(bys)
        if bys is then:
            for one in streams:
                one.return_far(first)
        for one in streams:
            one.far_ready(bys)
        for one, value in zip(streams, work(streams[0].far(bys))):
            put_at(one.partial, one.far(bys), value)
            for by in bys:
                one.far_back(by).start()
    for one in streams:
        one.return_far(then)


class Spread:
    def __init__(self, wide, packed, in_pieces, out_pieces, attn, w_in, w_out, sems):
        self.wide = wide
        self.packed, self.in_pieces, self.out_pieces = packed, in_pieces, out_pieces
        self.attn, self.w_in, self.w_out = attn, w_in, w_out
        (self.own_sem, self.z_s, self.z_r, self.plane_s, self.plane_r, self.core_s, self.core_r,
         self.in_s, self.in_r, self.out_s, self.out_r, self.own_in, self.own_out) = sems
        self.core, self.column, self.place = lax.axis_index("section"), lax.axis_index("expert"), lax.axis_index("shard")
        self.owners, self.pieces = lax.axis_size("expert"), lax.axis_size("shard")

    def spot(self, column, place):
        rows = self.packed.shape[0]
        return pl.ds(pl.multiple_of((column * self.pieces + place) * rows, rows), rows)

    def column_by(self, by):
        return lax.rem(self.column + by + self.owners, self.owners)

    def place_by(self, by):
        return lax.rem(self.place + by + self.pieces, self.pieces)

    def copy(self, source, target, send, recv, device):
        return pltpu.make_async_remote_copy(source, target, send, recv, device_id=device, device_id_type=MESH)

    def own(self):
        return pltpu.make_async_copy(self.packed, self.attn.at[self.core, self.spot(self.column, self.place)], self.own_sem)

    def along(self, by):
        block = self.attn.at[self.core, self.spot(self.column, self.place)]
        return self.copy(self.packed, block, self.z_s.at[by], self.z_r.at[by], (self.core, self.column, self.place_by(by)))

    def along_in(self, by):
        block = self.attn.at[self.core, self.spot(self.column, self.place_by(-by))]
        return self.copy(self.packed, block, self.z_s.at[by], self.z_r.at[by], (self.core, self.column, self.place_by(-by)))

    def plane(self, back, by):
        block = self.attn.at[self.core, self.spot(self.column, self.place_by(-back))]
        source = self.packed if back == 0 else block
        return self.copy(
            source, block, self.plane_s.at[back, by], self.plane_r.at[back, by], (self.core, self.column_by(by), self.place)
        )

    def plane_in(self, back, by):
        block = self.attn.at[self.core, self.spot(self.column_by(-by), self.place_by(-back))]
        return self.copy(
            block, block, self.plane_s.at[back, by], self.plane_r.at[back, by], (self.core, self.column_by(-by), self.place)
        )

    def over(self, back, by, section):
        block = self.attn.at[section, self.spot(self.column_by(-by), self.place_by(-back))]
        source = self.packed if back == 0 and by == 0 else block
        return self.copy(
            source, block, self.core_s.at[back, by], self.core_r.at[back, by], (1 - self.core, self.column, self.place)
        )

    def begin(self):
        self.own().start()
        for by in range(1, self.pieces):
            self.along(by).start()
        for by in range(1, self.owners):
            self.plane(0, by).start()
        self.over(0, 0, self.core).start()

    def pass_on(self):
        for back in range(1, self.pieces):
            self.along_in(back).wait_recv()
            for by in range(1, self.owners):
                self.plane(back, by).start()
            self.over(back, 0, self.core).start()

    def pass_over(self):
        for back in range(self.pieces):
            for by in range(1, self.owners):
                self.plane_in(back, by).wait_recv()
                self.over(back, by, self.core).start()
        self.own().wait()

    def over_ready(self):
        for back in range(self.pieces):
            for by in range(self.owners):
                self.over(back, by, 1 - self.core).wait_recv()

    def finish_attn(self):
        for by in range(1, self.pieces):
            self.along(by).wait_send()
        for back in range(self.pieces):
            for by in range(1, self.owners):
                self.plane(back, by).wait_send()
            for by in range(self.owners):
                self.over(back, by, self.core).wait_send()

    def in_rows(self, place):
        rows = self.w_in.shape[1] // self.pieces
        return pl.ds(pl.multiple_of(place * rows, rows), rows)

    def out_rows(self, place):
        rows = self.out_pieces.shape[1]
        return pl.ds(pl.multiple_of(lax.div(place, 2) * rows, rows), rows)

    def parts(self, core, place, section, rows):
        if not self.wide:
            return [(self.in_pieces.at[core, lax.rem(place, 2)], self.w_in.at[section, rows])]
        hidden = self.in_pieces.shape[1] // 2
        half = self.out_pieces.shape[1]
        pairs = []
        for pair in range(self.pieces // 2):
            for side in range(2):
                for ahead in range(0, half, CHUNK):
                    at = side * hidden + (2 * pair + lax.rem(place, 2)) * 2 * half + core * half + ahead
                    to = 2 * (pair * half + ahead) + side * CHUNK
                    pairs.append((
                        self.in_pieces.at[:, pl.ds(pl.multiple_of(at, CHUNK), CHUNK)],
                        self.w_in.at[section, rows, pl.ds(to, CHUNK)],
                    ))
        return pairs

    def in_copies(self, cross, by):
        core = 1 - self.core if cross else self.core
        place = self.place_by(by)
        return [
            self.copy(source, target, self.in_s.at[cross, by, i], self.in_r.at[cross, by, i], (core, self.column, place))
            for i, (source, target) in enumerate(self.parts(core, place, self.core, self.in_rows(self.place)))
        ]

    def in_here(self, cross, by):
        core = 1 - self.core if cross else self.core
        place = self.place_by(-by)
        return [
            self.copy(source, target, self.in_s.at[cross, by, i], self.in_r.at[cross, by, i], (core, self.column, place))
            for i, (source, target) in enumerate(self.parts(self.core, self.place, core, self.in_rows(place)))
        ]

    def out_copy(self, cross, by):
        core = 1 - self.core if cross else self.core
        return self.copy(
            self.out_pieces.at[core], self.w_out.at[self.core, self.out_rows(self.place)],
            self.out_s.at[cross, by // 2], self.out_r.at[cross, by // 2], (core, self.column, self.place_by(by)),
        )

    def out_here(self, cross, by):
        core = 1 - self.core if cross else self.core
        place = self.place_by(-by)
        return self.copy(
            self.out_pieces.at[core], self.w_out.at[core, self.out_rows(place)],
            self.out_s.at[cross, by // 2], self.out_r.at[cross, by // 2], (core, self.column, place),
        )

    def own_pieces(self):
        copies = [
            pltpu.make_async_copy(source, target, self.own_in.at[i])
            for i, (source, target) in enumerate(self.parts(self.core, self.place, self.core, self.in_rows(self.place)))
        ]
        return copies + [
            pltpu.make_async_copy(
                self.out_pieces.at[self.core], self.w_out.at[self.core, self.out_rows(self.place)], self.own_out
            )
        ]

    def expert_routes(self):
        for by in range(self.pieces):
            for cross in (0, 1):
                if by or cross:
                    yield cross, by

    def begin_experts(self, evens=(0, 1)):
        if 1 in evens:
            for one in self.own_pieces():
                one.start()
        for cross, by in self.expert_routes():
            if (by + 1) % 2 not in evens:
                continue
            for one in self.in_copies(cross, by):
                one.start()
            if by % 2 == 0:
                self.out_copy(cross, by).start()

    def experts_ready(self, cross):
        for way, by in self.expert_routes():
            if way == cross:
                for one in self.in_here(cross, by):
                    one.wait_recv()
                if by % 2 == 0:
                    self.out_here(cross, by).wait_recv()
        if not cross:
            for one in self.own_pieces():
                one.wait()

    def finish_experts(self):
        for cross, by in self.expert_routes():
            for one in self.in_copies(cross, by):
                one.wait_send()
            if by % 2 == 0:
                self.out_copy(cross, by).wait_send()


def spread_scratch(owners, pieces, parts):
    dma = pltpu.SemaphoreType.DMA
    return [dma, dma((pieces,)), dma((pieces,))] + [dma((pieces, owners))] * 4 + [
        dma((2, pieces, parts)), dma((2, pieces, parts)), dma((2, pieces // 2)), dma((2, pieces // 2)), dma((parts,)), dma,
    ]


def place_of():
    return lax.axis_index("section"), lax.axis_index("expert"), lax.axis_index("shard")


def remote(source, target, send, recv, device):
    return pltpu.make_async_remote_copy(source, target, send, recv, device_id=device, device_id_type=MESH)


class ExpertSum:
    def __init__(self, grad_in, grad_out, got_even, got_odd, got_out, sems):
        self.grad_in, self.grad_out = grad_in, grad_out
        self.got_even, self.got_odd, self.got_out = got_even, got_odd, got_out
        self.in_s, self.in_r, self.out_s, self.out_r = sems
        self.core, self.column, self.place = place_of()
        self.pieces = lax.axis_size("shard")

    def place_by(self, by):
        return lax.rem(self.place + by + self.pieces, self.pieces)

    def in_rows(self, place):
        rows = self.grad_in.shape[0] // self.pieces
        return pl.ds(pl.multiple_of(place * rows, rows), rows)

    def out_rows(self, place):
        rows = self.grad_out.shape[0] // (self.pieces // 2)
        return pl.ds(pl.multiple_of(lax.div(place, 2) * rows, rows), rows)

    def in_copy(self, by, way):
        place = self.place_by(way * by)
        target = self.got_even.at[by // 2 - 1] if by % 2 == 0 else self.got_odd.at[by // 2]
        return remote(
            self.grad_in.at[self.in_rows(place)], target, self.in_s.at[by - 1], self.in_r.at[by - 1],
            (self.core, self.column, place),
        )

    def out_copy(self, by, way):
        place = self.place_by(way * by)
        at = by // 2 - 1
        return remote(
            self.grad_out.at[self.out_rows(place)], self.got_out.at[at], self.out_s.at[at], self.out_r.at[at],
            (self.core, self.column, place),
        )

    def even(self, way=1):
        return [self.in_copy(by, way) for by in range(2, self.pieces, 2)]

    def odd(self, way=1):
        copies = [self.in_copy(by, way) for by in range(1, self.pieces, 2)]
        return copies + [self.out_copy(by, way) for by in range(2, self.pieces, 2)]


def start_all(copies):
    for one in copies:
        one.start()


def wait_all(sent, arriving):
    for one in arriving:
        one.wait_recv()
    for one in sent:
        one.wait_send()


def expert_sum_sems(pieces):
    dma = pltpu.SemaphoreType.DMA
    return [dma((pieces - 1,)), dma((pieces - 1,)), dma((max(pieces // 2 - 1, 1),)), dma((max(pieces // 2 - 1, 1),))]


def got_shapes(pieces, in_rows, columns, out_rows, width):
    spare = max(pieces // 2 - 1, 1)
    return (
        shaped((spare, in_rows, columns), BF16), shaped((pieces // 2, in_rows, columns), BF16),
        shaped((spare, out_rows, width), BF16),
    )


def greet_these(devices):
    barrier = pltpu.get_barrier_semaphore()
    for device in devices:
        pl.semaphore_signal(barrier, inc=1, device_id=device, device_id_type=MESH)
    pl.semaphore_wait(barrier, len(devices))


def along_z():
    core, column, place = place_of()
    pieces = lax.axis_size("shard")
    return [(core, column, lax.rem(place + by, pieces)) for by in range(1, pieces)]


def in_plane():
    core, column, place = place_of()
    owners = lax.axis_size("expert")
    return [(core, lax.rem(column + by, owners), place) for by in range(1, owners)]


def other_core():
    core, column, place = place_of()
    return [(1 - core, column, place)]


def load_weights(attn, section, w, small, sems):
    width = w.shape[0]
    first = pltpu.make_async_copy(attn.at[section, :, pl.ds(4 * width, LANES)], small, sems.at[0])
    then = pltpu.make_async_copy(attn.at[section], w, sems.at[1])
    first.start()
    then.start()
    first.wait()
    return then


class AttnSum:
    def __init__(self, grads, buffers, sems):
        self.grads = grads
        self.from_core, self.summed, self.from_plane, self.through, self.from_z = buffers
        self.core_s, self.core_r, self.plane_s, self.plane_r, self.z_s, self.z_r = sems
        self.core, self.column, self.place = place_of()
        self.owners, self.pieces = lax.axis_size("expert"), lax.axis_size("shard")

    def block(self, column, k, core):
        rows = self.summed.shape[2]
        return pl.ds(pl.multiple_of((column * self.pieces + 2 * k + core) * rows, rows), rows)

    def each(self):
        return [(column, k) for column in range(self.owners) for k in range(self.pieces // 2)]

    def to_core(self, column, k):
        return remote(
            self.grads.at[self.block(column, k, 1 - self.core)], self.from_core.at[column, k], self.core_s.at[column, k],
            self.core_r.at[column, k], (1 - self.core, self.column, self.place),
        )

    def to_plane(self, by, way=1):
        column = lax.rem(self.column + way * by + self.owners, self.owners)
        return remote(
            self.summed.at[column], self.from_plane.at[by - 1], self.plane_s.at[by - 1], self.plane_r.at[by - 1],
            (self.core, column, self.place),
        )

    def place_by(self, by):
        return lax.rem(self.place + by + self.pieces, self.pieces)

    def along(self, by, way=1):
        place = self.place_by(way * by)
        return remote(
            self.through.at[lax.div(place, 2)], self.from_z.at[by - 1], self.z_s.at[by - 1], self.z_r.at[by - 1],
            (self.core, self.column, place),
        )

    def holds(self, place):
        return lax.rem(place, 2) == self.core

    def start(self):
        for column, k in self.each():
            self.to_core(column, k).start()

    def add_cores(self):
        for column, k in self.each():
            self.to_core(column, k).wait_recv()
        for column, k in self.each():
            own = self.grads[self.block(column, k, self.core), :]
            self.summed[column, k] = (own.astype(F32) + self.from_core[column, k].astype(F32)).astype(BF16)
        for by in range(1, self.owners):
            self.to_plane(by).start()

    def plane_ready(self):
        for by in range(1, self.owners):
            self.to_plane(by, -1).wait_recv()

    def add_plane(self):
        total = self.summed[self.column].astype(F32)
        for by in range(1, self.owners):
            total = total + self.from_plane[by - 1].astype(F32)
        self.through[...] = total.astype(BF16)
        for by in range(1, self.pieces):

            @pl.when(self.holds(self.place_by(by)))
            def _():
                self.along(by).start()

    def z_ready(self):
        @pl.when(self.holds(self.place))
        def _():
            for by in range(1, self.pieces):
                self.along(by, -1).wait_recv()

    def add_z(self, target):
        @pl.when(self.holds(self.place))
        def _():
            total = self.through[lax.div(self.place, 2)].astype(F32)
            for by in range(1, self.pieces):
                total = total + self.from_z[by - 1].astype(F32)
            target[...] = total

    def finish_near(self):
        for column, k in self.each():
            self.to_core(column, k).wait_send()
        for by in range(1, self.owners):
            self.to_plane(by).wait_send()

    def finish_z(self):
        for by in range(1, self.pieces):

            @pl.when(self.holds(self.place_by(by)))
            def _():
                self.along(by).wait_send()


def attn_sum_scratch(owners, pieces, rows, columns):
    blocks = (owners, pieces // 2, rows, columns)
    dma = pltpu.SemaphoreType.DMA
    return [
        pltpu.VMEM(blocks, BF16), pltpu.VMEM(blocks, BF16), pltpu.VMEM((owners - 1,) + blocks[1:], BF16),
        pltpu.VMEM(blocks[1:], BF16), pltpu.VMEM((pieces - 1,) + blocks[2:], BF16),
    ], [dma(blocks[:2])] * 2 + [dma((owners - 1,))] * 2 + [dma((pieces - 1,))] * 2


def column_devices():
    core, column, place = place_of()
    pieces = lax.axis_size("shard")
    return [
        (one, column, lax.rem(place + by, pieces))
        for by in range(pieces)
        for one in (core, 1 - core)
    ][1:]


def column_of(row):
    return jnp.broadcast_to(row.astype(F32), (LANES, row.shape[1])).T[:, :1]


def tables_of(seg_row, cosine, sine):
    seq_len = seg_row.shape[1]
    seg_col = column_of(seg_row).astype(jnp.int32)
    start = jnp.sum(jnp.where(seg_row < seg_col, 1.0, 0.0), axis=1, keepdims=True)
    place = lax.broadcasted_iota(jnp.int32, (seq_len, LANES), 0).astype(F32)
    lane = lane_of(seq_len)
    rate = jnp.exp((lane % (HEAD // 2)).astype(F32) * (-2.0 * math.log(10000.0) / HEAD))
    angles = (place - start) * rate
    cosine[...] = jnp.cos(angles)
    sine[...] = jnp.where(lane % HEAD < HEAD // 2, -jnp.sin(angles), jnp.sin(angles))
    return seg_col


def front_kernel(dims, inside, wide, n):
    width = n.x_in.shape[2]
    core, column, place = place_of()
    nexp, owners = dims[1], lax.axis_size("expert")
    packed_w = n.packed_w
    if inside:
        packed_w[:, : 3 * width] = n.w_qkv[...]
        packed_w[:, 3 * width : 4 * width] = n.w_attn[...]
        rows = packed_w.shape[0]
        n.turning[...] = jnp.zeros(n.turning.shape, F32)
        for array, at in ((n.router, 0), (n.const_proj, AT_PROJ), (n.const_vec, AT_VEC), (n.gains, AT_GAIN)):
            n.turning[at : at + array.shape[0], :rows] = array[...].astype(F32)
        packed_w[:, 4 * width :] = n.turning[:, :LANES].T[:rows].astype(BF16)
    spread = Spread(wide, packed_w, n.in_pieces, n.w_out_here, n.attn if inside else None, n.w_in, n.w_out, n.spread_sems)
    first, second = core == 0, core == 1
    tokens = Exchange(0, n.buffer_0, n.arrived, *n.token_home, n.made, n.sems)
    tokens_1 = Exchange(1, n.buffer_0, n.groups_1, *n.token_home, n.made, n.sems)
    grads_1 = Exchange(2, n.buffer_2, n.groups_2, *n.grad_home, n.returned, n.sems)
    greet_these(column_devices() + in_plane())

    @pl.when(first)
    def _():
        if inside:
            spread.begin()

    sibling = (1 - core, column, place)
    n.mix_own[...] = jnp.zeros(n.mix_own.shape, F32)
    n.mix_own[:nexp, :nexp] = n.gate_mix[...]
    crossing = [
        remote(n.routes.at[1 - core], n.routes_all.at[core], n.cross_s.at[0], n.cross_r.at[0], sibling),
        remote(n.priority.at[1 - core], n.prio.at[core], n.cross_s.at[1], n.cross_r.at[1], sibling),
        remote(n.mix_own, n.mix.at[core], n.cross_s.at[2], n.cross_r.at[2], sibling),
    ]
    arriving = [
        remote(n.routes.at[core], n.routes_all.at[1 - core], n.cross_s.at[0], n.cross_r.at[0], sibling),
        remote(n.priority.at[core], n.prio.at[1 - core], n.cross_s.at[1], n.cross_r.at[1], sibling),
        remote(n.mix_own, n.mix.at[1 - core], n.cross_s.at[2], n.cross_r.at[2], sibling),
    ]
    start_all(crossing)
    bring = [
        pltpu.make_async_copy(n.x_in.at[core], n.x, n.bring_sems.at[0]),
        pltpu.make_async_copy(n.cotangent.at[core], n.upstream, n.bring_sems.at[1]),
    ]
    attn = (n.attn.at[0], n.attn.at[1])
    if not inside:
        attn = (n.attn_here, n.attn_here)
        loads = [pltpu.make_async_copy(n.attn.at[section], n.attn_here, n.bring_sems.at[2]) for section in range(2)]
        bring.append(loads[0])
    start_all(bring)
    seg_row = n.segments[core]
    seg_col = tables_of(seg_row, n.cosine, n.sine)
    n.routes_all[core] = n.routes[core]
    n.prio[core] = n.priority[core]
    n.mix[core] = n.mix_own[...]
    n.turning[...] = jnp.zeros(n.turning.shape, F32)
    n.turning[:nexp, :] = n.gate_prev[core].astype(F32)
    n.r[...] = n.turning[...].T.astype(BF16)
    wait_all(crossing, arriving)
    lane = lane_of(n.ints.shape[1])
    for section in range(2):
        routes = n.routes_all[section]
        first_route, second_route = (column_of(routes[k : k + 1]).astype(jnp.int32) for k in range(TOP))
        n.ints[section] = jnp.where(lane == 0, first_route, second_route)
    for one in bring:
        one.wait()

    @pl.when(first)
    def _():
        if inside:
            spread.pass_on()
        spread.begin_experts()
        if inside:
            spread.pass_over()

    @pl.when(second)
    def _():
        if inside:
            spread.over_ready()

    keep = [
        pltpu.make_async_copy(source, target, n.keep_sems.at[section, i])
        for section, targets in enumerate(((n.qkv_0, n.probs_0), (n.qkv_1, n.probs_1)))
        for i, (source, target) in enumerate(zip((n.qkv_here, n.probs_here), targets))
    ]
    leaving = [pltpu.make_async_copy(n.w_in.at[0], n.w_in_kept, n.leave_sems.at[0]),
               pltpu.make_async_copy(n.w_out.at[0], n.w_out_kept, n.leave_sems.at[1])]
    if inside:
        leaving += [
            pltpu.make_async_copy(n.attn.at[section], n.attn_kept.at[section], n.leave_sems.at[2 + section])
            for section in range(2)
        ]
    n.small[0] = attn[0][:, 4 * width :]
    attend_kernel(
        dims, n.x, n.r, attn[0], n.small.at[0], n.mix.at[0], n.cosine, n.sine, seg_col, seg_row,
        n.ints.at[0], n.prio.at[0],
        n.after_0, n.qkv_here, n.probs_here, n.attended_0, n.packed_0, n.slots_0, n.r_next, n.buffer_0,
    )
    tokens.start()
    start_all(keep[:2])
    if not inside:
        loads[1].start()

    @pl.when(second)
    def _():
        if inside:
            spread.begin()

    tokens.spread()

    @pl.when(first)
    def _():
        spread.experts_ready(0)

    @pl.when(second)
    def _():
        if inside:
            spread.pass_on()
        spread.experts_ready(1)
        spread.begin_experts((1,))

    tokens.near_ready()
    put_near(tokens.partial, made_by(near_rows(tokens.groups), n.w_in.at[0], n.w_out.at[0]))
    tokens.near_back().start()
    exchange_far([tokens], lambda picks: [made_by(rows_at(tokens.groups, picks), n.w_in.at[0], n.w_out.at[0])])

    @pl.when(second)
    def _():
        if inside:
            spread.pass_over()
        spread.begin_experts((0,))

    tokens.near_arrived()
    tokens.return_home(range(owners))
    tokens.finish_dispatch()
    tokens.finish()
    if inside:

        @pl.when(first)
        def _():
            spread.over_ready()

    if not inside:
        loads[1].wait()
    n.small[1] = attn[1][:, 4 * width :]
    for one in keep[:2]:
        one.wait()
    middle_kernel(
        dims, n.after_0, n.packed_0, n.slots_0, n.ints.at[0], tokens.result, n.small.at[0],
        n.r_next, attn[1], n.small.at[1], n.mix.at[1], n.cosine, n.sine, seg_col, seg_row,
        n.ints.at[1], n.prio.at[1], n.upstream,
        n.out_0, n.picked_0, n.after_1, n.qkv_here, n.probs_here, n.attended_1, n.packed_1, n.slots_1, n.buffer_0, n.buffer_2,
    )
    start_all(keep[2:])
    both = (tokens_1, grads_1)
    for one in both:
        one.start()
    for one in both:
        one.spread()

    @pl.when(first)
    def _():
        spread.experts_ready(1)

    @pl.when(second)
    def _():
        spread.experts_ready(0)

    w_in, w_out = n.w_in.at[1], n.w_out.at[1]
    start_all(leaving)
    for one in both:
        one.near_ready()
    parts = both_ways(
        near_rows(tokens_1.groups), near_rows(grads_1.groups), w_in, w_out, near_of(n.hidden), near_of(n.grad_both)
    )
    for one, part in zip(both, parts):
        put_near(one.partial, part)
        one.near_back().start()
    exchange_far(
        both,
        lambda picks: both_ways(
            rows_at(tokens_1.groups, picks), rows_at(grads_1.groups, picks), w_in, w_out,
            far_of(n.hidden, picks), far_of(n.grad_both, picks),
        ),
    )
    n.grad_out[...] = mm(all_rows(n.hidden), all_rows(grads_1.groups), TN).astype(BF16)
    for one in both:
        one.near_arrived()
        one.return_home(range(owners))
    weight_grads_in(all_rows(tokens_1.groups), n.grad_both, n.grad_in)
    for one in both:
        one.finish_dispatch()
        one.finish()
    for one in keep[2:] + leaving:
        one.wait()
    if inside:
        spread.finish_attn()
    spread.finish_experts()


def turn_kernel(dims, inside, n):
    sums = ExpertSum(n.grad_in_1, n.grad_out_1, n.even, n.odd, n.got_out, n.sum_sems)
    loading = load_weights(n.attn, 1, n.w, n.small, n.load_sems)
    expert_loads = [
        pltpu.make_async_copy(n.w_in_all, n.w_in, n.load_sems.at[2]),
        pltpu.make_async_copy(n.w_out_all, n.w_out, n.load_sems.at[3]),
    ]
    start_all(expert_loads)
    grads = Exchange(0, n.buffer, n.groups, *n.home, n.blocks_back, n.sems)
    attn = []
    if inside:
        attn = [AttnSum(n.grads_a, n.attn_buffers_a, n.attn_sems_a), AttnSum(n.grads_b, n.attn_buffers_b, n.attn_sems_b)]
    greet_these(other_core() + along_z() + in_plane())
    start_all(sums.even())
    _, gain_second, vec_rows = small_rows_of(n.small)
    n.out[...] = combine(
        n.after[...], n.packed[...], n.slots[...], n.ints[1], n.made, gain_second, vec_rows, dims, n.picked
    ).astype(BF16)

    def rows_done():
        give_back(n.grad_x[...].astype(BF16).astype(F32), n.packed_0[...], n.slots_0[...], dims, n.buffer)
        grads.start()

    hooks = types.SimpleNamespace(
        early=False, rows_done=rows_done, first_done=lambda: [one.start() for one in attn[:1]],
        second_done=lambda: [one.start() for one in attn[1:]],
    )
    back_body(
        dims, n.upstream, None, n.after, n.packed, n.slots, n.ints.at[1], n.picked, n.returned, n.r, n.w, n.small, n.mix.at[1],
        n.x, n.qkv, n.probs, n.attended, n.cosine, n.sine, n.grad_x, n.grad_r, n.grad_mix, (n.grads_a, n.grads_b),
        n.grad_qkv, loading, hooks,
    )
    for one in expert_loads:
        one.wait()
    forward_again(near_rows(n.arrived), n.w_in, n.w_out, near_of(n.both), near_of(n.hidden))
    grads.spread()
    start_all(sums.odd())
    for one in attn:
        one.add_cores()
    grads.near_ready()

    def near_both(columns):
        return n.both[:2, :, :, columns].reshape(near_count, 2 * CHUNK)

    near_count = n.both.shape[0] // 2 * n.both.shape[1] * n.both.shape[2]
    put_near(
        grads.partial, back_of(near_rows(grads.groups), n.w_in, n.w_out, near_both, near_of(n.grad_both))
    )
    grads.near_back().start()
    for bys in grads.steps():
        picks = grads.far(bys)
        forward_again(
            rows_at(n.arrived, picks), n.w_in, n.w_out, far_of(n.both, picks), far_of(n.hidden, picks)
        )
    exchange_far(
        [grads],
        lambda picks: [back_of(
            rows_at(grads.groups, picks), n.w_in, n.w_out, lambda columns: rows_at(n.both, picks, columns),
            far_of(n.grad_both, picks),
        )],
    )
    n.grad_out_0[...] = mm(all_rows(n.hidden), all_rows(grads.groups), TN).astype(BF16)
    for one in attn:
        one.plane_ready()
        one.add_plane()
    grads.near_arrived()
    grads.return_home(range(grads.owners))
    weight_grads_in(all_rows(n.arrived), n.grad_both, n.grad_in_0)
    grads.finish_dispatch()
    grads.finish()
    for one, target in zip(attn, (n.attn_sum_a, n.attn_sum_b)):
        one.finish_near()
        one.z_ready()
        one.add_z(target)
        one.finish_z()
    wait_all(sums.even() + sums.odd(), sums.even(-1) + sums.odd(-1))


def spread_columns(target, halves_at, hidden_here):
    rows, columns = target.shape
    hidden = columns // 2
    pieces = hidden // (2 * hidden_here)
    parity = lax.rem(lax.axis_index("shard"), 2)
    for first_parity in range(2):

        @pl.when(parity == first_parity)
        def _():
            for half in range(2):
                for q in range(2):
                    odd = first_parity if q == 0 else 1 - first_parity
                    for pair in range(pieces // 2):
                        for side in range(2):
                            for ahead in range(0, hidden_here, CHUNK):
                                at = side * hidden + (2 * pair + odd) * 2 * hidden_here + half * hidden_here + ahead
                                source = 2 * (pair * hidden_here + ahead) + side * CHUNK
                                target[:, at : at + CHUNK] = halves_at(half, q)[:, source : source + CHUNK].astype(F32)


def last_kernel(dims, inside, wide, n):
    core, column, place = place_of()
    pieces = lax.axis_size("shard")
    pair_count = pieces // 2
    (sibling,) = other_core()
    loading = load_weights(n.attn, 0, n.w, n.small, n.load_sems)
    sums = ExpertSum(n.grad_in_0, n.grad_out_0, n.even_0, n.odd_0, n.got_out_0, n.sum_sems)
    attn = []
    if inside:
        attn = [AttnSum(n.grads_a, n.attn_buffers_a, n.attn_sems_a), AttnSum(n.grads_b, n.attn_buffers_b, n.attn_sems_b)]
    greet_these(other_core() + along_z() + (in_plane() if inside else []))
    start_all(sums.even() + sums.odd())
    pairs = ((n.out_0, n.out_1, n.both_out), (n.grad_x_0, n.grad_x_1, n.both_x), (n.grad_r_0, n.grad_r_1, n.r_pair))

    def swaps(section):
        for i, (zero, one, both) in enumerate(pairs):
            own, other = (zero, one) if section == 0 else (one, zero)
            yield (
                remote(other, both.at[section], n.swap_s.at[i], n.swap_r.at[i], sibling),
                pltpu.make_async_copy(own, both.at[section], n.local_sem.at[i]),
            )

    def each_core(action):
        for section in range(2):

            @pl.when(core == section)
            def _():
                action(section)

    def add_experts(section, grad_in, grad_out, even, odd, got_out):
        rows, out_rows = even.shape[1], got_out.shape[1]
        own_in = grad_in[pl.ds(pl.multiple_of(place * rows, rows), rows), :]
        own_out = grad_out[pl.ds(pl.multiple_of(lax.div(place, 2) * out_rows, out_rows), out_rows), :]
        in_sum = [own_in.astype(F32), odd[0].astype(F32)]
        for i in range(pair_count - 1):
            in_sum[0] = in_sum[0] + even[i].astype(F32)
            in_sum[1] = in_sum[1] + odd[i + 1].astype(F32)
        out_sum = own_out.astype(F32)
        for i in range(pair_count - 1):
            out_sum = out_sum + got_out[i].astype(F32)

        @pl.when(core == section)
        def _():
            for q in range(2):
                n.in_mine[q] = in_sum[q]
            n.out_mine[...] = out_sum

        @pl.when(core != section)
        def _():
            for q in range(2):
                n.in_sent[q] = in_sum[q].astype(BF16)
            n.out_sent[...] = out_sum.astype(BF16)
            for one in finals:
                one.start()

    finals = [
        remote(n.in_sent, n.in_got, n.final_s.at[0], n.final_r.at[0], sibling),
        remote(n.out_sent, n.out_got, n.final_s.at[1], n.final_r.at[1], sibling),
    ]
    hooks = types.SimpleNamespace(
        early=True, first_done=lambda: [one.start() for one in attn[:1]],
        heads_done=lambda: [one.add_cores() for one in attn[:1]], second_done=lambda: [one.start() for one in attn[1:]],
    )
    back_body(
        dims, n.grad_x_1, n.grad_r_1, n.after, n.packed, n.slots, n.ints.at[0], n.picked, n.returned, n.r, n.w, n.small,
        n.mix.at[0], n.x, n.qkv, n.probs, n.attended, n.cosine, n.sine, n.grad_x_0, n.grad_r_0, n.grad_mix,
        (n.grads_a, n.grads_b), n.grad_qkv, loading, hooks,
    )

    @each_core
    def _(section):
        for away, here in swaps(section):
            away.start()
            here.start()

    for one in attn[1:]:
        one.add_cores()
    add_experts(1, n.grad_in_1, n.grad_out_1, n.even_1, n.odd_1, n.got_out_1)
    for one in attn:
        one.plane_ready()
        one.add_plane()
    wait_all(sums.even() + sums.odd(), sums.even(-1) + sums.odd(-1))
    add_experts(0, n.grad_in_0, n.grad_out_0, n.even_0, n.odd_0, n.got_out_0)
    for one in finals:
        one.wait()
    for half in range(2):

        @pl.when(core == half)
        def _():
            if wide:
                hidden_here = n.out_mine.shape[0]
                spread_columns(n.in_total, lambda at, q: n.in_mine[q] if at == half else n.in_got[q], hidden_here)
            else:
                for q in range(2):
                    n.in_total[half, q] = n.in_mine[q]
                    n.in_total[1 - half, q] = n.in_got[q].astype(F32)
            count = n.out_mine.shape[0]
            n.out_total[half * count : (half + 1) * count] = n.out_mine[...]
            n.out_total[(1 - half) * count : (2 - half) * count] = n.out_got[...].astype(F32)

    for i, (one, sum_0, sum_1, total) in enumerate(zip(
        attn, (n.attn_sum_0a, n.attn_sum_0b), (n.attn_sum_1a, n.attn_sum_1b), (n.attn_total_a, n.attn_total_b)
    )):
        one.z_ready()
        one.add_z(sum_0)
        holder = one.holds(place)
        for section in range(2):
            mine, other = (sum_0, sum_1) if section == 0 else (sum_1, sum_0)
            home = remote(other, total, n.final_s.at[2 + i], n.final_r.at[2 + i], sibling)

            @pl.when(holder & (core == section))
            def _():
                home.start()
                total[...] = mine[...]
                home.wait_send()

            @pl.when(jnp.logical_not(holder) & (core == section))
            def _():
                home.wait_recv()

    if inside:
        width = n.x.shape[1]
        half = width // LANES // 2 * LANES
        for batch, total in enumerate((n.attn_total_a, n.attn_total_b)):
            for part in range(3):
                at = part * width + batch * half
                n.qkv_total[:, at : at + half] = total[:, part * half : (part + 1) * half]
        n.attn_out_total[...] = n.attn_total_a[:, 3 * half :]
        small = n.attn_total_b[:, 3 * half :]
        nexp, rows = n.mix_total.shape[0], small.shape[0]
        n.mix_total[...] = small[:nexp, AT_MIX : AT_MIX + nexp]
        n.turning[...] = jnp.zeros(n.turning.shape, F32)
        n.turning[:rows] = small
        turned_small = n.turning[...].T
        for target, at in ((n.router_total, 0), (n.proj_total, AT_PROJ), (n.vec_total, AT_VEC), (n.gain_total, AT_GAIN)):
            target[...] = turned_small[at : at + target.shape[0], :rows]

    @each_core
    def _(section):
        for away, here in swaps(section):
            away.wait()
            here.wait()

    for batch in range(2):
        n.both_r[batch] = n.r_pair[batch].T[: n.both_r.shape[1]]

    for one in attn:
        one.finish_near()
        one.finish_z()


def local(
    x_in,
    cotangent,
    gate_prev,
    segments,
    routes,
    priority,
    attn_qkv,
    attn_out,
    router,
    const_proj,
    const_vec,
    gains,
    gate_mix,
    expert_in,
    expert_out,
):
    seq_len, width = x_in.shape[2:]
    nexp = gate_prev.shape[-1]
    owners, pieces = lax.axis_size("expert"), lax.axis_size("shard")
    nffn = owners * expert_in.shape[1]
    nconst = const_vec.shape[-1]
    capacity = (5 * TOP * seq_len + 4 * nexp - 1) // (4 * nexp)
    room = -(-capacity // 16) * 16
    slots = nffn * room
    core = lax.axis_index("section")
    first_core = core == 0
    in_rows, columns = expert_in.shape[2:]
    hidden_here = expert_out.shape[2] // 2
    pairs = pieces // 2
    quarter = pairs * hidden_here
    chunks = quarter // CHUNK
    rows = attn_qkv.shape[1]
    inside, wide = rows % 16 == 0, hidden_here % CHUNK == 0

    def swap(item):
        return lax.ppermute(item, "section", [(0, 1), (1, 0)])

    def by_section(own, other):
        return jnp.where(first_core, own, other), jnp.where(first_core, other, own)

    def as_chunks(half):
        half = jnp.moveaxis(half, 3, 0).reshape(2, in_rows, 2, chunks, CHUNK)
        return jnp.swapaxes(half, 2, 3).reshape(2, in_rows, 2 * quarter)

    w_out = expert_out[0, 0].reshape(2, hidden_here, width)
    in_pieces = expert_in[0, 0]
    if not wide:
        w_in = in_pieces.reshape(in_rows, 2, pairs, 2, 2, hidden_here)
        in_pieces = jnp.stack([as_chunks(w_in[:, :, :, :, half]) for half in range(2)])
    given = None
    if not inside:
        def lanes(array, upto):
            return jnp.pad(array, ((0, 0), (0, upto - array.shape[1])))

        small = [
            lanes(router[0], AT_PROJ), lanes(const_proj[0], AT_VEC - AT_PROJ), lanes(const_vec[0], AT_GAIN - AT_VEC),
            lanes(gains[0], LANES - AT_GAIN),
        ]
        shared = jnp.concatenate([attn_qkv[0], attn_out[0]] + small, axis=1)
        shared = lax.all_gather(shared, ("expert", "shard"), axis=0, tiled=True)
        given = jnp.stack(by_section(shared, swap(shared)))
    dims = (nffn, nexp, capacity, slots, rows if inside else 0)
    heads = width // HEAD
    blocks = (owners, room, width)
    token_f32 = shaped((seq_len, width), F32)
    token_b16 = shaped((seq_len, width), BF16)
    lanes_f32 = shaped((seq_len, LANES), F32)
    lanes_i32 = shaped((seq_len, LANES), jnp.int32)
    block_shape = shaped(blocks, BF16)
    attn_shape = shaped((width, 4 * width + LANES), BF16)
    attn_columns = attn_shape.shape[1]
    pair_shape = shaped((TOP, seq_len, width), BF16)
    in_shape, out_shape = shaped((width, 2 * quarter), BF16), shaped((quarter, width), BF16)
    dma = pltpu.SemaphoreType.DMA
    even, odd, got_out = got_shapes(pieces, in_rows, 2 * quarter, hidden_here, width)

    def vmem(shape):
        return pltpu.VMEM(shape.shape, shape.dtype)

    def attend_out(section):
        return {
            f"after_{section}": token_f32,
            f"qkv_{section}": shaped((seq_len, 3 * width), BF16),
            f"probs_{section}": shaped((heads, seq_len, seq_len), BF16),
            f"attended_{section}": token_b16,
            f"packed_{section}": lanes_f32,
            f"slots_{section}": lanes_i32,
        }

    ins = dict(
        in_pieces=in_pieces, w_out_here=w_out, x_in=x_in[:, 0], cotangent=cotangent[:, 0], gate_prev=jnp.swapaxes(gate_prev[:, 0], 1, 2),
        segments=segments, routes=jnp.swapaxes(routes[0, :, 0], 1, 2), priority=priority[0], gate_mix=gate_mix[0],
    )
    table_shapes = dict(
        mix=shaped((2, LANES, LANES), F32), cosine=lanes_f32, sine=lanes_f32, ints=shaped((2, seq_len, LANES), jnp.int32),
    )
    outs = dict(
        w_in_kept=in_shape, w_out_kept=out_shape, arrived=shaped((4,) + blocks, BF16), r_next=shaped((seq_len, LANES), BF16), out_0=token_b16, picked_0=pair_shape,
        made=block_shape, returned=block_shape, grad_in=in_shape, grad_out=out_shape, **attend_out(0), **attend_out(1),
        x=token_b16, r=shaped((seq_len, LANES), BF16), upstream=token_f32, **table_shapes,
    )
    if inside:
        outs["attn_kept"] = shaped((2,) + attn_shape.shape, BF16)
        ins = dict(
            ins, w_qkv=attn_qkv[0], w_attn=attn_out[0], router=router[0].T, const_proj=const_proj[0].T,
            const_vec=const_vec[0].T, gains=gains[0].T,
        )
    else:
        ins["attn"] = given
    f = call(
        lambda n: front_kernel(dims, inside, wide, n), 0, ins, outs,
        dict(
            small=pltpu.VMEM((2, width, LANES), BF16), buffer_0=vmem(block_shape),
            buffer_2=vmem(block_shape), groups_1=pltpu.VMEM((4,) + blocks, BF16), groups_2=pltpu.VMEM((4,) + blocks, BF16),
            token_home=home_buffers(*blocks), grad_home=home_buffers(*blocks), sems=exchange_sems(3, owners),
            spread_sems=spread_scratch(owners, pieces, 2 * pairs * max(hidden_here // CHUNK, 1) if wide else 1),
            packed_w=pltpu.VMEM((rows, 4 * width + LANES), BF16), mix_own=pltpu.VMEM((LANES, LANES), F32),
            prio=pltpu.VMEM((2, 1, seq_len), jnp.int32), cross_s=dma((3,)), cross_r=dma((3,)), bring_sems=dma((3,)),
            qkv_here=pltpu.VMEM((seq_len, 3 * width), BF16), probs_here=pltpu.VMEM((heads, seq_len, seq_len), BF16),
            keep_sems=dma((2, 2)), leave_sems=dma((4,)),
            w_in=pltpu.VMEM((2, width, 2 * quarter), BF16), w_out=pltpu.VMEM((2, quarter, width), BF16),
            **(dict(attn=pltpu.VMEM((2,) + attn_shape.shape, BF16)) if inside else dict(attn_here=vmem(attn_shape))), turning=pltpu.VMEM((LANES, seq_len), F32), routes_all=pltpu.VMEM((2, TOP, seq_len), jnp.int32),
            hidden=pltpu.VMEM((4,) + blocks[:2] + (quarter,), BF16), grad_both=pltpu.VMEM((4,) + blocks[:2] + (2 * quarter,), BF16),
        ),
        ("in_pieces", "w_out_here", "x_in", "cotangent", "qkv_0", "probs_0", "qkv_1", "probs_1")
        + ("w_in_kept", "w_out_kept", "attn_kept" if inside else "attn"), 8 << 30,
    )
    tables = dict(mix=f.mix, cosine=f.cosine, sine=f.sine, ints=f.ints)
    attn_all = f.attn_kept if inside else given
    scratch = dict(
        w=vmem(attn_shape), small=pltpu.VMEM((width, LANES), BF16), load_sems=dma((4,)), grad_qkv=pltpu.VMEM((seq_len, 3 * width), BF16),
        sum_sems=expert_sum_sems(pieces),
    )
    attn_scratch = {}
    half = width // LANES // 2 * LANES
    batches = dict(a=3 * half + width, b=3 * half + LANES)
    block_sums = {name: shaped((rows, lanes) if inside else (8, LANES), F32) for name, lanes in batches.items()}
    grad_shapes = {f"grads_{name}": shaped((width, lanes), BF16) for name, lanes in batches.items()}
    if inside:
        for name, lanes in batches.items():
            buffers, sems = attn_sum_scratch(owners, pieces, rows, lanes)
            attn_scratch.update({f"attn_buffers_{name}": buffers, f"attn_sems_{name}": sems})
    outs = dict(
        out=token_b16, grad_x=token_f32, grad_r=lanes_f32, grad_mix=shaped((LANES, LANES), F32), even=even, odd=odd,
        got_out=got_out, grad_in_0=in_shape, grad_out_0=out_shape, blocks_back=block_shape,
        attn_sum_a=block_sums["a"], attn_sum_b=block_sums["b"],
    )
    more = {name: vmem(shape) for name, shape in grad_shapes.items()}
    if not inside:
        outs, more = dict(outs, **grad_shapes), {}
    t = call(
        lambda n: turn_kernel(dims, inside, n), 1,
        dict(
            attn=attn_all, w_in_all=f.w_in_kept, w_out_all=f.w_out_kept, grad_in_1=f.grad_in, grad_out_1=f.grad_out,
            upstream=f.upstream, after=f.after_1, packed=f.packed_1, slots=f.slots_1, made=f.made, returned=f.returned, r=f.r_next,
            x=f.out_0, qkv=f.qkv_1, probs=f.probs_1, attended=f.attended_1, packed_0=f.packed_0, slots_0=f.slots_0,
            arrived=f.arrived, **tables,
        ),
        outs,
        dict(
            picked=vmem(pair_shape), buffer=vmem(block_shape), groups=pltpu.VMEM((4,) + blocks, BF16), home=home_buffers(*blocks),
            sems=exchange_sems(1, owners), w_in=vmem(in_shape), w_out=vmem(out_shape),
            both=pltpu.VMEM((4,) + blocks[:2] + (2 * quarter,), F32 if slots <= 384 else BF16), hidden=pltpu.VMEM((4,) + blocks[:2] + (quarter,), BF16),
            grad_both=pltpu.VMEM((4,) + blocks[:2] + (2 * quarter,), BF16), **scratch, **attn_scratch, **more,
        ),
        ("attn", "w_in_all", "w_out_all", "grad_in_1", "grad_out_1"), 12 << 30,
    )
    in_total = shaped((in_rows, columns) if wide else (2, 2, in_rows, 2 * quarter), F32)
    half_in, half_out = (2, in_rows, 2 * quarter), (hidden_here, width)
    outs = dict(
        both_out=shaped((2, seq_len, width), BF16), both_x=shaped((2, seq_len, width), F32),
        both_r=shaped((2, nexp, seq_len), F32), in_total=in_total, out_total=shaped((2 * hidden_here, width), F32),
        grad_mix=shaped((LANES, LANES), F32),
    )
    if inside:
        narrow = dict(router_total=nexp, proj_total=const_proj.shape[2], vec_total=nconst, gain_total=2)
        outs = dict(
            outs, qkv_total=shaped((rows, 3 * width), F32), attn_out_total=shaped((rows, width), F32),
            mix_total=shaped((nexp, nexp), F32), **{name: shaped((lanes, rows), F32) for name, lanes in narrow.items()},
        )
    else:
        outs = dict(outs, **grad_shapes)
    z = call(
        lambda n: last_kernel(dims, inside, wide, n), 2,
        dict(
            attn=attn_all, grad_in_0=t.grad_in_0, grad_out_0=t.grad_out_0, grad_in_1=f.grad_in, grad_out_1=f.grad_out,
            even_1=t.even, odd_1=t.odd, got_out_1=t.got_out, attn_sum_1a=t.attn_sum_a, attn_sum_1b=t.attn_sum_b, out_0=f.out_0, out_1=t.out,
            grad_x_1=t.grad_x, grad_r_1=t.grad_r, after=f.after_0, packed=f.packed_0, slots=f.slots_0, picked=f.picked_0,
            returned=t.blocks_back, r=f.r, x=f.x, qkv=f.qkv_0, probs=f.probs_0, attended=f.attended_0, **tables,
        ),
        outs,
        dict(
            even_0=vmem(even), odd_0=vmem(odd), got_out_0=vmem(got_out), grad_x_0=vmem(token_f32), grad_r_0=vmem(lanes_f32),
            attn_sum_0a=vmem(block_sums["a"]), attn_sum_0b=vmem(block_sums["b"]), attn_total_a=vmem(block_sums["a"]),
            attn_total_b=vmem(block_sums["b"]), turning=pltpu.VMEM((LANES, LANES), F32), r_pair=pltpu.VMEM((2, seq_len, LANES), F32), in_mine=pltpu.VMEM(half_in, F32), out_mine=pltpu.VMEM(half_out, F32),
            in_sent=pltpu.VMEM(half_in, BF16), out_sent=pltpu.VMEM(half_out, BF16), in_got=pltpu.VMEM(half_in, BF16),
            out_got=pltpu.VMEM(half_out, BF16), swap_s=dma((3,)), swap_r=dma((3,)), local_sem=dma((3,)), final_s=dma((4,)),
            final_r=dma((4,)), **scratch, **attn_scratch, **more,
        ),
        ("attn", "both_out", "both_x", "out_0", "out_1"), 6 << 30,
    )
    in_grad = z.in_total
    if not wide:
        odd = lax.axis_index("shard") % 2
        in_grad = jnp.where(odd == 0, in_grad, in_grad[:, ::-1])
        in_grad = jnp.swapaxes(in_grad.reshape(2, 2, in_rows, chunks, 2, CHUNK), 3, 4)
        in_grad = in_grad.reshape(2, 2, in_rows, 2, pairs, hidden_here)
        in_grad = jnp.transpose(in_grad, (2, 3, 4, 1, 0, 5)).reshape(in_rows, columns)
    if inside:
        shared_grads = (
            z.qkv_total, z.attn_out_total, z.router_total.T, z.proj_total.T, z.vec_total.T, z.gain_total.T, z.mix_total
        )
    else:
        def joined(a, b):
            parts = []
            for part in range(3):
                parts += [a[:, part * half : (part + 1) * half], b[:, part * half : (part + 1) * half]]
            return jnp.concatenate(parts + [a[:, 3 * half :], b[:, 3 * half :]], axis=1)

        grads_0, grads_1 = joined(z.grads_a, z.grads_b), joined(t.grads_a, t.grads_b)
        own = jnp.where(first_core, grads_0, grads_1)
        total = own.astype(F32) + swap(jnp.where(first_core, grads_1, grads_0)).astype(F32)
        total = lax.psum_scatter(total.astype(BF16), ("expert", "shard"), scatter_dimension=0, tiled=True).astype(F32)
        own = jnp.where(first_core, z.grad_mix, t.grad_mix)
        mix_grad = own + swap(jnp.where(first_core, t.grad_mix, z.grad_mix))
        small = total[:, 4 * width :]
        shared_grads = (
            total[:, : 3 * width],
            total[:, 3 * width : 4 * width],
            small[:, :nexp],
            small[:, AT_PROJ : AT_PROJ + const_proj.shape[-1]],
            small[:, AT_VEC : AT_VEC + nconst],
            small[:, AT_GAIN : AT_GAIN + 2],
            lax.psum(mix_grad, ("expert", "shard"))[:nexp, :nexp],
        )
    return (
        z.both_out[None, :, None],
        z.both_x[None, :, None],
        jnp.swapaxes(z.both_r, 1, 2)[None, :, None],
        *[grad[None] for grad in shared_grads],
        in_grad[None, None],
        z.out_total[None, None],
    )


def solution(mesh):
    placed = (
        P(None, ("expert", "shard"), None, None),
        P(None, ("expert", "shard"), None, None),
        P(None, ("expert", "shard"), None, None),
        P(None, ("expert", "shard"), None),
        P("section", None, ("expert", "shard"), None, None),
        P("section", None, ("expert", "shard"), None),
        P("section", ("expert", "shard"), None),
        P("section", ("expert", "shard"), None),
        P("section", ("expert", "shard"), None),
        P("section", ("expert", "shard"), None),
        P("section", ("expert", "shard"), None),
        P("section", ("expert", "shard"), None),
        P("section", None, None),
        P("section", "expert", "shard", None),
        P("section", "expert", "shard", None),
    )
    return jax.shard_map(
        local,
        mesh=mesh,
        in_specs=placed,
        out_specs=(
            P("section", None, ("expert", "shard"), None, None),
            P("section", None, ("expert", "shard"), None, None),
            P("section", None, ("expert", "shard"), None, None),
            P("section", ("expert", "shard"), None),
            P("section", ("expert", "shard"), None),
            P("section", ("expert", "shard"), None),
            P("section", ("expert", "shard"), None),
            P("section", ("expert", "shard"), None),
            P("section", ("expert", "shard"), None),
            P("section", None, None),
            P("section", "expert", "shard", None),
            P("section", "expert", "shard", None),
        ),
        check_vma=False,
    )
```

profile of v0, /device:TPU:0, one launch (start us, length us, event | category | flops | bytes accessed | tf_op | source)
XLA Modules:
  0.0 379.6 jit_solution(10601577569010048560)
XLA Ops:
  0.7 198.9 %shard_map.238 = (bf16[768,1024]{1,0:T(8,128)(2,1)}, bf16[512,768]{1,0:T(8,128)(2,1)}, bf16[4,4,80,768]{3,2,1,0:T(8,128)(2,1)}, bf16[256,128]{1,0:T(8,128)(2,1)}...) custom-call(bf16[192,4096]{1,0:T(8,128)(2,1)} %bitcast.66, ...), custom_call_target="tpu_custom_call" | custom-call | flops 8589934592 | bytes 41943040 | tf_op jit(solution)/shard_map/pallas_call | solution.py:379
  199.5 89.5 %shard_map.239 = (bf16[256,768]{1,0:T(8,128)(2,1)}, f32[256,768]{1,0:T(8,128)}, f32[256,128]{1,0:T(8,128)}, f32[128,128]{1,0:T(8,128)}, bf16[1,192,1024]{2,1,0:T...) custom-call(bf16[2,768,3200]{2,1,0:T(8,128)(2,1)} %get-tuple-element, ...), custom_call_target="tpu_custom_call" | custom-call | flops 12884901888 | bytes 41943040 | tf_op jit(solution)/shard_map/pallas_call | solution.py:379
  289.0 78.0 %shard_map.240 = (bf16[2,256,768]{2,1,0:T(8,128)(2,1)}, f32[2,256,768]{2,1,0:T(8,128)}, f32[2,8,256]{2,1,0:T(8,128)}, f32[192,4096]{1,0:T(8,128)}, f32[512,768]{...) custom-call(bf16[2,768,3200]{2,1,0:T(8,128)(2,1)} %get-tuple-element, ...), custom_call_target="tpu_custom_call" | custom-call | flops 6442450944 | bytes 41943040 | tf_op jit(solution)/shard_map/pallas_call | solution.py:379
  367.1 0.0 copy-start.2
  367.1 0.0 copy-start.5
  367.1 0.0 copy-start.3
  367.1 2.2 copy.42
  369.3 0.0 copy-done.2
  369.4 1.1 copy.43
  370.5 0.6 copy.44
  371.1 0.0 copy-done.3
  371.1 0.8 copy.45
  371.9 0.0 copy-done.4
  371.9 0.7 copy.46
  372.6 0.6 copy.47
  373.2 0.0 copy-done.8
  373.2 0.6 copy.48
  373.7 0.6 copy.49
  374.3 0.6 copy.50
  374.9 0.0 copy-done.6
  374.9 0.6 copy.51
  375.5 1.7 copy.52
  377.1 0.9 copy-done.1
  378.0 1.1 copy.53
  (13 shorter events, 0.0 us)
Async XLA Ops:
  367.1 2.2 copy-start.2
  367.1 3.4 copy-start.5
  367.1 4.0 %copy-start.3 = (f32[48,2304]{1,0:T(8,128)S(1)}, f32[48,2304]{1,0:T(8,128)}, u32[]{:S(2)}) copy-start(f32[48,2304]{1,0:T(8,128)} %get-tuple-element.109) | copy-start | bytes 1327108
  369.3 2.6 copy-start.4
  369.3 3.2 copy-start.7
  369.3 3.8 %copy-start.8 = (f32[4,48]{1,0:T(4,128)S(1)}, f32[4,48]{1,0:T(4,128)}, u32[]{:S(2)}) copy-start(f32[4,48]{1,0:T(4,128)} %get-tuple-element.112) | copy-start | bytes 2308
  369.3 4.4 %copy-start.10 = (f32[2,48]{1,0:T(2,128)S(1)}, f32[2,48]{1,0:T(2,128)}, u32[]{:S(2)}) copy-start(f32[2,48]{1,0:T(2,128)} %get-tuple-element.113) | copy-start | bytes 1156
  369.3 5.0 %copy-start.9 = (f32[2,48]{1,0:T(2,128)S(1)}, f32[2,48]{1,0:T(2,128)}, u32[]{:S(2)}) copy-start(f32[2,48]{1,0:T(2,128)} %get-tuple-element.114) | copy-start | bytes 1156
  369.4 5.5 %copy-start.6 = (f32[8,8]{1,0:T(8,128)S(1)}, f32[8,8]{1,0:T(8,128)}, u32[]{:S(2)}) copy-start(f32[8,8]{1,0:T(8,128)} %get-tuple-element.115) | copy-start | bytes 772
  369.4 6.1 %copy-start = (f32[192,4096]{1,0:T(8,128)S(1)}, f32[192,4096]{1,0:T(8,128)}, u32[]{:S(2)}) copy-start(f32[192,4096]{1,0:T(8,128)} %get-tuple-element.116) | copy-start | bytes 9437188
  375.5 2.5 copy-start.1
where the time goes:
time: 387 us; the launch traced here: 380 us
  Pallas kernels  366 us (95%)
  local copies, waits for them, and re-layouts  12 us (3%)
    pallas_call x3, Pallas kernels, call(): pl.pallas_call(body, out_shape=list(outs.values()), in_specs=spaces(ins),...  366 us
    unnamed x34, local copies, waits for them, and re-layouts  12 us

commit v1 on v0

--- a/solution.py
+++ b/solution.py
@@ -707,13 +707,32 @@
     def own(self):
         return pltpu.make_async_copy(self.packed, self.attn.at[self.core, self.spot(self.column, self.place)], self.own_sem)
 
-    def along(self, by):
-        block = self.attn.at[self.core, self.spot(self.column, self.place)]
-        return self.copy(self.packed, block, self.z_s.at[by], self.z_r.at[by], (self.core, self.column, self.place_by(by)))
-
-    def along_in(self, by):
-        block = self.attn.at[self.core, self.spot(self.column, self.place_by(-by))]
-        return self.copy(self.packed, block, self.z_s.at[by], self.z_r.at[by], (self.core, self.column, self.place_by(-by)))
+    def along(self, back, way):
+        block = self.attn.at[self.core, self.spot(self.column, self.place_by(-back))]
+        there = back + 1 if way else (back - 1) % self.pieces
+        return self.copy(
+            self.packed if back == 0 else block, block, self.z_s.at[way, back], self.z_r.at[there],
+            (self.core, self.column, self.place_by(1 if way else -1)),
+        )
+
+    def hand_on(self, back, action):
+        if back < self.pieces - 1:
+
+            @pl.when((self.place >= back) & (self.place < self.pieces - 1))
+            def _():
+                action(self.along(back, 1))
+
+        if back != 1:
+
+            @pl.when((self.place > 0) if back == 0 else (self.place > 0) & (self.place < back))
+            def _():
+                action(self.along(back, 0))
+
+    def along_in(self, back):
+        block = self.attn.at[self.core, self.spot(self.column, self.place_by(-back))]
+        return self.copy(
+            block, block, self.z_s.at[1, back], self.z_r.at[back], (self.core, self.column, self.place_by(-1))
+        )
 
     def plane(self, back, by):
         block = self.attn.at[self.core, self.spot(self.column, self.place_by(-back))]
@@ -737,18 +756,28 @@
 
     def begin(self):
         self.own().start()
-        for by in range(1, self.pieces):
-            self.along(by).start()
+        self.hand_on(0, lambda copy: copy.start())
         for by in range(1, self.owners):
             self.plane(0, by).start()
         self.over(0, 0, self.core).start()
 
     def pass_on(self):
-        for back in range(1, self.pieces):
+        def arrived(back):
             self.along_in(back).wait_recv()
+            self.hand_on(back, lambda copy: copy.start())
             for by in range(1, self.owners):
                 self.plane(back, by).start()
             self.over(back, 0, self.core).start()
+
+        for far in range(1, self.pieces):
+
+            @pl.when(self.place >= far)
+            def _():
+                arrived(far)
+
+            @pl.when(self.place + far < self.pieces)
+            def _():
+                arrived(self.pieces - far)
 
     def pass_over(self):
         for back in range(self.pieces):
@@ -763,8 +792,8 @@
                 self.over(back, by, 1 - self.core).wait_recv()
 
     def finish_attn(self):
-        for by in range(1, self.pieces):
-            self.along(by).wait_send()
+        for back in range(self.pieces):
+            self.hand_on(back, lambda copy: copy.wait_send())
         for back in range(self.pieces):
             for by in range(1, self.owners):
                 self.plane(back, by).wait_send()
@@ -877,7 +906,7 @@
 
 def spread_scratch(owners, pieces, parts):
     dma = pltpu.SemaphoreType.DMA
-    return [dma, dma((pieces,)), dma((pieces,))] + [dma((pieces, owners))] * 4 + [
+    return [dma, dma((2, pieces)), dma((pieces,))] + [dma((pieces, owners))] * 4 + [
         dma((2, pieces, parts)), dma((2, pieces, parts)), dma((2, pieces // 2)), dma((2, pieces // 2)), dma((parts,)), dma,
     ]
 

time: 387 us -> 376 us (0.972)
  Pallas kernels: 366 us -> 357 us
    pallas_call x3, Pallas kernels: 366 us -> 357 us  [call(): pl.pallas_call(body, out_shape=list(outs.values()), in_specs=spaces(ins),...]
where the time goes in v1:
time: 376 us; the launch traced here: 370 us
  Pallas kernels  357 us (95%)
  local copies, waits for them, and re-layouts  12 us (3%)
    pallas_call x3, Pallas kernels, call(): pl.pallas_call(body, out_shape=list(outs.values()), in_specs=spaces(ins),...  357 us
    unnamed x34, local copies, waits for them, and re-layouts  12 us

profile of v1, /device:TPU:0, one launch (start us, length us, event | category | flops | bytes accessed | tf_op | source)
XLA Modules:
  0.0 369.8 jit_solution(1023615914495449804)
XLA Ops:
  0.7 190.9 %shard_map.238 = (bf16[768,1024]{1,0:T(8,128)(2,1)}, bf16[512,768]{1,0:T(8,128)(2,1)}, bf16[4,4,80,768]{3,2,1,0:T(8,128)(2,1)}, bf16[256,128]{1,0:T(8,128)(2,1)}...) custom-call(bf16[192,4096]{1,0:T(8,128)(2,1)} %bitcast.66, ...), custom_call_target="tpu_custom_call" | custom-call | flops 8589934592 | bytes 41943040 | tf_op jit(solution)/shard_map/pallas_call | solution.py:379
  191.5 87.9 %shard_map.239 = (bf16[256,768]{1,0:T(8,128)(2,1)}, f32[256,768]{1,0:T(8,128)}, f32[256,128]{1,0:T(8,128)}, f32[128,128]{1,0:T(8,128)}, bf16[1,192,1024]{2,1,0:T...) custom-call(bf16[2,768,3200]{2,1,0:T(8,128)(2,1)} %get-tuple-element, ...), custom_call_target="tpu_custom_call" | custom-call | flops 12884901888 | bytes 41943040 | tf_op jit(solution)/shard_map/pallas_call | solution.py:379
  279.4 77.9 %shard_map.240 = (bf16[2,256,768]{2,1,0:T(8,128)(2,1)}, f32[2,256,768]{2,1,0:T(8,128)}, f32[2,8,256]{2,1,0:T(8,128)}, f32[192,4096]{1,0:T(8,128)}, f32[512,768]{...) custom-call(bf16[2,768,3200]{2,1,0:T(8,128)(2,1)} %get-tuple-element, ...), custom_call_target="tpu_custom_call" | custom-call | flops 6442450944 | bytes 41943040 | tf_op jit(solution)/shard_map/pallas_call | solution.py:379
  357.3 0.0 copy-start.2
  357.3 0.0 copy-start.5
  357.3 0.0 copy-start.3
  357.3 2.2 copy.42
  359.5 0.0 copy-done.2
  359.6 1.1 copy.43
  360.7 0.0 copy-done.5
  360.7 0.6 copy.44
  361.3 0.0 copy-done.3
  361.3 0.8 copy.45
  362.1 0.7 copy.46
  362.8 0.6 copy.47
  363.4 0.6 copy.48
  363.9 0.6 copy.49
  364.5 0.0 copy-done.9
  364.5 0.6 copy.50
  365.1 0.0 copy-done.6
  365.1 0.6 copy.51
  365.7 1.7 copy.52
  367.3 0.9 copy-done.1
  368.2 1.1 copy.53
  (13 shorter events, 0.0 us)
Async XLA Ops:
  357.3 2.2 copy-start.2
  357.3 3.4 copy-start.5
  357.3 4.0 %copy-start.3 = (f32[48,2304]{1,0:T(8,128)S(1)}, f32[48,2304]{1,0:T(8,128)}, u32[]{:S(2)}) copy-start(f32[48,2304]{1,0:T(8,128)} %get-tuple-element.109) | copy-start | bytes 1327108
  359.5 2.6 copy-start.4
  359.5 3.2 copy-start.7
  359.5 3.8 %copy-start.8 = (f32[4,48]{1,0:T(4,128)S(1)}, f32[4,48]{1,0:T(4,128)}, u32[]{:S(2)}) copy-start(f32[4,48]{1,0:T(4,128)} %get-tuple-element.112) | copy-start | bytes 2308
  359.5 4.4 %copy-start.10 = (f32[2,48]{1,0:T(2,128)S(1)}, f32[2,48]{1,0:T(2,128)}, u32[]{:S(2)}) copy-start(f32[2,48]{1,0:T(2,128)} %get-tuple-element.113) | copy-start | bytes 1156
  359.6 5.0 %copy-start.9 = (f32[2,48]{1,0:T(2,128)S(1)}, f32[2,48]{1,0:T(2,128)}, u32[]{:S(2)}) copy-start(f32[2,48]{1,0:T(2,128)} %get-tuple-element.114) | copy-start | bytes 1156
  359.6 5.5 %copy-start.6 = (f32[8,8]{1,0:T(8,128)S(1)}, f32[8,8]{1,0:T(8,128)}, u32[]{:S(2)}) copy-start(f32[8,8]{1,0:T(8,128)} %get-tuple-element.115) | copy-start | bytes 772
  359.6 6.1 %copy-start = (f32[192,4096]{1,0:T(8,128)S(1)}, f32[192,4096]{1,0:T(8,128)}, u32[]{:S(2)}) copy-start(f32[192,4096]{1,0:T(8,128)} %get-tuple-element.116) | copy-start | bytes 9437188
  365.7 2.5 copy-start.1

commit v2 on v1

--- a/solution.py
+++ b/solution.py
@@ -959,7 +959,10 @@
 
     def odd(self, way=1):
         copies = [self.in_copy(by, way) for by in range(1, self.pieces, 2)]
-        return copies + [self.out_copy(by, way) for by in range(2, self.pieces, 2)]
+        return copies + self.down(way)
+
+    def down(self, way=1):
+        return [self.out_copy(by, way) for by in range(2, self.pieces, 2)]
 
 
 def start_all(copies):
@@ -1232,6 +1235,7 @@
     def _():
         if inside:
             spread.over_ready()
+            spread.begin()
 
     keep = [
         pltpu.make_async_copy(source, target, n.keep_sems.at[section, i])
@@ -1256,11 +1260,6 @@
     if not inside:
         loads[1].start()
 
-    @pl.when(second)
-    def _():
-        if inside:
-            spread.begin()
-
     tokens.spread()
 
     @pl.when(first)
@@ -1366,7 +1365,7 @@
     if inside:
         attn = [AttnSum(n.grads_a, n.attn_buffers_a, n.attn_sems_a), AttnSum(n.grads_b, n.attn_buffers_b, n.attn_sems_b)]
     greet_these(other_core() + along_z() + in_plane())
-    start_all(sums.even())
+    start_all(sums.even() + sums.odd()[: -len(sums.down()) or None])
     _, gain_second, vec_rows = small_rows_of(n.small)
     n.out[...] = combine(
         n.after[...], n.packed[...], n.slots[...], n.ints[1], n.made, gain_second, vec_rows, dims, n.picked
@@ -1389,7 +1388,7 @@
         one.wait()
     forward_again(near_rows(n.arrived), n.w_in, n.w_out, near_of(n.both), near_of(n.hidden))
     grads.spread()
-    start_all(sums.odd())
+    start_all(sums.down())
     for one in attn:
         one.add_cores()
     grads.near_ready()

time: 376 us -> 368 us (0.979)
  Pallas kernels: 357 us -> 348 us
    pallas_call x3, Pallas kernels: 357 us -> 348 us  [call(): pl.pallas_call(body, out_shape=list(outs.values()), in_specs=spaces(ins),...]
where the time goes in v2:
time: 368 us; the launch traced here: 362 us
  Pallas kernels  348 us (95%)
  local copies, waits for them, and re-layouts  12 us (3%)
    pallas_call x3, Pallas kernels, call(): pl.pallas_call(body, out_shape=list(outs.values()), in_specs=spaces(ins),...  348 us
    unnamed x34, local copies, waits for them, and re-layouts  12 us

profile of v2, /device:TPU:0, one launch (start us, length us, event | category | flops | bytes accessed | tf_op | source)
XLA Modules:
  0.0 361.6 jit_solution(2275365265666932995)
XLA Ops:
  0.7 190.5 %shard_map.238 = (bf16[768,1024]{1,0:T(8,128)(2,1)}, bf16[512,768]{1,0:T(8,128)(2,1)}, bf16[4,4,80,768]{3,2,1,0:T(8,128)(2,1)}, bf16[256,128]{1,0:T(8,128)(2,1)}...) custom-call(bf16[192,4096]{1,0:T(8,128)(2,1)} %bitcast.66, ...), custom_call_target="tpu_custom_call" | custom-call | flops 8589934592 | bytes 41943040 | tf_op jit(solution)/shard_map/pallas_call | solution.py:379
  191.2 79.1 %shard_map.239 = (bf16[256,768]{1,0:T(8,128)(2,1)}, f32[256,768]{1,0:T(8,128)}, f32[256,128]{1,0:T(8,128)}, f32[128,128]{1,0:T(8,128)}, bf16[1,192,1024]{2,1,0:T...) custom-call(bf16[2,768,3200]{2,1,0:T(8,128)(2,1)} %get-tuple-element, ...), custom_call_target="tpu_custom_call" | custom-call | flops 12884901888 | bytes 41943040 | tf_op jit(solution)/shard_map/pallas_call | solution.py:379
  270.3 78.8 %shard_map.240 = (bf16[2,256,768]{2,1,0:T(8,128)(2,1)}, f32[2,256,768]{2,1,0:T(8,128)}, f32[2,8,256]{2,1,0:T(8,128)}, f32[192,4096]{1,0:T(8,128)}, f32[512,768]{...) custom-call(bf16[2,768,3200]{2,1,0:T(8,128)(2,1)} %get-tuple-element, ...), custom_call_target="tpu_custom_call" | custom-call | flops 6442450944 | bytes 41943040 | tf_op jit(solution)/shard_map/pallas_call | solution.py:379
  349.1 0.0 copy-start.2
  349.1 0.0 copy-start.5
  349.1 0.0 copy-start.3
  349.1 2.2 copy.42
  351.3 0.0 copy-done.2
  351.3 0.0 copy-start.10
  351.4 1.1 copy.43
  352.5 0.0 copy-done.5
  352.5 0.6 copy.44
  353.1 0.8 copy.45
  353.9 0.7 copy.46
  354.6 0.6 copy.47
  355.1 0.6 copy.48
  355.7 0.0 copy-done.10
  355.7 0.6 copy.49
  356.3 0.0 copy-done.9
  356.3 0.6 copy.50
  356.9 0.6 copy.51
  357.5 1.7 copy.52
  359.1 0.9 copy-done.1
  360.0 1.1 copy.53
  (13 shorter events, 0.0 us)
Async XLA Ops:
  349.1 2.2 copy-start.2
  349.1 3.4 copy-start.5
  349.1 4.0 %copy-start.3 = (f32[48,2304]{1,0:T(8,128)S(1)}, f32[48,2304]{1,0:T(8,128)}, u32[]{:S(2)}) copy-start(f32[48,2304]{1,0:T(8,128)} %get-tuple-element.109) | copy-start | bytes 1327108
  351.3 2.6 copy-start.4
  351.3 3.2 copy-start.7
  351.3 3.8 %copy-start.8 = (f32[4,48]{1,0:T(4,128)S(1)}, f32[4,48]{1,0:T(4,128)}, u32[]{:S(2)}) copy-start(f32[4,48]{1,0:T(4,128)} %get-tuple-element.112) | copy-start | bytes 2308
  351.3 4.4 %copy-start.10 = (f32[2,48]{1,0:T(2,128)S(1)}, f32[2,48]{1,0:T(2,128)}, u32[]{:S(2)}) copy-start(f32[2,48]{1,0:T(2,128)} %get-tuple-element.113) | copy-start | bytes 1156
  351.3 5.0 %copy-start.9 = (f32[2,48]{1,0:T(2,128)S(1)}, f32[2,48]{1,0:T(2,128)}, u32[]{:S(2)}) copy-start(f32[2,48]{1,0:T(2,128)} %get-tuple-element.114) | copy-start | bytes 1156
  351.3 5.5 %copy-start.6 = (f32[8,8]{1,0:T(8,128)S(1)}, f32[8,8]{1,0:T(8,128)}, u32[]{:S(2)}) copy-start(f32[8,8]{1,0:T(8,128)} %get-tuple-element.115) | copy-start | bytes 772
  351.4 6.1 %copy-start = (f32[192,4096]{1,0:T(8,128)S(1)}, f32[192,4096]{1,0:T(8,128)}, u32[]{:S(2)}) copy-start(f32[192,4096]{1,0:T(8,128)} %get-tuple-element.116) | copy-start | bytes 9437188
  357.5 2.5 copy-start.1
